TPU v7x, 256 devices: a whole 4x4x8 slice. The times are simulated.
256 devices in a mesh: comp: 16 (over y, z_hi), freq: 16 (over z_lo, x, core).
Axes of the slice: x: 4, y: 4, z: 8 (z_hi: 4, z_lo: 2; z = z_hi * 2 + z_lo), core: 2. Of those that a mesh axis runs over, the one named last changes fastest.
Arguments:
- station_uvw: float32 [3, 512], replicated, may hold values from -1792 to 1792
- directions: float32 [2, 4096], P(None, 'comp'), may hold values from -0.1 to 0.1
- flux_ref: float32 [4096], P('comp'), may hold values from 0.2 to 2
- spectral_index: float32 [4096], P('comp'), may hold values from -1.5 to 0.5
- channel_index: int32 [32], P('freq'), may hold values from 0 to 4095
- slot_pair: int32 [528], replicated, may hold values from 0 to 527, each once
- observed: float32 [32, 528, 512], P('freq', 'comp'), may hold values from -6 to 6
Outputs:
- residual: float32 [32, 528, 512], P('freq', 'comp')
- flux_grad: float32 [4096], P('comp')
Inputs may be any that keep to these rules, and one draw needn't show every extreme that they name: slot_pair[k] is the pair index held at slot k; every pair is held once; slots k * 33 to (k + 1) * 33 - 1 lie on index k of comp.
All inputs are finite; a program needn't handle non-finite values.
Results may differ from a plain program's by a relative error of at most 0.0059.
Values sent between devices are 32-bit elements; how exact they have to be, the bound alone decides.
No kernel may reach another device: no remote copies, remote signals or barrier semaphores. Data moves between devices by JAX's collectives and lax.ppermute only.
A program may use at most 128 MiB of HBM per device.

v0:
```python
import math

import jax
import jax.numpy as jnp
import numpy as np
from jax import lax
from jax.sharding import PartitionSpec as P

NB = 32


def pair_tables(blocks):
    first, second = np.triu_indices(blocks)
    row_ids = np.arange(blocks)[:, None]
    col_ids = np.arange(blocks)[None, :]
    low_ids = np.minimum(row_ids, col_ids)
    high_ids = np.maximum(row_ids, col_ids)
    grid = low_ids * blocks - low_ids * (low_ids - 1) // 2 + high_ids - low_ids
    return (first.astype(np.int32), second.astype(np.int32), grid.astype(np.int32))


def slot_blocks(slot_pair, blocks):
    first, second, grid = pair_tables(blocks)
    count = first.shape[0]
    match = slot_pair[:, None] == jnp.arange(count, dtype=jnp.int32)[None, :]
    row_block = jnp.sum(jnp.where(match, jnp.asarray(first)[None, :], 0), axis=1).astype(jnp.int32)
    col_block = jnp.sum(jnp.where(match, jnp.asarray(second)[None, :], 0), axis=1).astype(jnp.int32)
    return (row_block, col_block)


def phasor_pair(station_uvw, directions, freq_ratio):
    l_part = directions[0]
    m_part = directions[1]
    w_term = jnp.sqrt(1.0 - l_part * l_part - m_part * m_part) - 1.0
    path_len = (
        station_uvw[0][:, None] * l_part[None, :]
        + station_uvw[1][:, None] * m_part[None, :]
        + station_uvw[2][:, None] * w_term[None, :]
    )
    angles = 2.0 * math.pi * freq_ratio * path_len
    return (jnp.cos(angles).astype(jnp.bfloat16), (-jnp.sin(angles)).astype(jnp.bfloat16))


def model_matrix(weighted_re, weighted_im, phase_re, phase_im):
    stations = phase_re.shape[0]
    left = jnp.concatenate(
        [
            jnp.concatenate([weighted_re, weighted_im], axis=1),
            jnp.concatenate([weighted_im, -weighted_re], axis=1),
        ],
        axis=0,
    )
    right = jnp.concatenate([phase_re, phase_im], axis=1)
    stacked_model = lax.dot_general(
        left, right, (((1,), (1,)), ((), ())), preferred_element_type=jnp.float32
    )
    return (stacked_model[:stations], stacked_model[stations:])


def pick_blocks(matrix, row_block, col_block, blocks, side_len):
    block_grid = matrix.reshape(blocks, side_len, blocks, side_len).transpose(0, 2, 1, 3)
    block_grid = block_grid.reshape(blocks * blocks, side_len, side_len)
    return block_grid[row_block * blocks + col_block]


def residual_blocks(model_re, model_im, observed, on_diag, side_len):
    shaped = observed.reshape(observed.shape[:-1] + (2, side_len, side_len))
    above = jnp.arange(side_len)[:, None] < jnp.arange(side_len)[None, :]
    part_re = jnp.where(above, shaped[..., 0, :, :], 0.0)
    part_im = jnp.where(above, shaped[..., 1, :, :], 0.0)
    herm_re = part_re + jnp.swapaxes(part_re, -1, -2)
    herm_im = part_im - jnp.swapaxes(part_im, -1, -2)
    flag = on_diag[:, None, None]
    ref_re = jnp.where(flag, herm_re, shaped[..., 0, :, :])
    ref_im = jnp.where(flag, herm_im, shaped[..., 1, :, :])
    autos = flag & (jnp.arange(side_len)[:, None] == jnp.arange(side_len)[None, :])
    res_re = jnp.where(autos, 0.0, model_re - ref_re)
    res_im = jnp.where(autos, 0.0, model_im - ref_im)
    flat_shape = res_re.shape[:-2] + (side_len * side_len,)
    return jnp.concatenate([res_re.reshape(flat_shape), res_im.reshape(flat_shape)], axis=-1)


def hermitian_matrix(slot_rows, slot_pair, blocks, side_len):
    first, second, grid = pair_tables(blocks)
    chans = slot_rows.shape[0]
    canonical = jnp.zeros_like(slot_rows).at[:, slot_pair].set(slot_rows)
    arranged = canonical[:, jnp.asarray(grid.reshape(-1))]
    arranged = arranged.reshape(chans, blocks, blocks, 2, side_len, side_len)
    below = jnp.asarray(np.arange(blocks)[:, None] > np.arange(blocks)[None, :])[
        None, :, :, None, None
    ]
    part_re = jnp.where(below, jnp.swapaxes(arranged[:, :, :, 0], -1, -2), arranged[:, :, :, 0])
    part_im = jnp.where(below, -jnp.swapaxes(arranged[:, :, :, 1], -1, -2), arranged[:, :, :, 1])
    total = blocks * side_len
    matrix_re = part_re.transpose(0, 1, 3, 2, 4).reshape(chans, total, total)
    matrix_im = part_im.transpose(0, 1, 3, 2, 4).reshape(chans, total, total)
    return (matrix_re, matrix_im)


def contract(matrix_re, matrix_im, phase_re, phase_im):
    top_half = jnp.concatenate([matrix_re, -matrix_im], axis=1)
    bottom_half = jnp.concatenate([matrix_im, matrix_re], axis=1)
    stacked = jnp.concatenate([phase_re, phase_im], axis=0)
    product = jnp.dot(
        jnp.concatenate([top_half, bottom_half], axis=0),
        stacked,
        preferred_element_type=jnp.float32,
    )
    return jnp.sum(stacked.astype(jnp.float32) * product, axis=0)


def body(station_uvw, directions, flux_ref, spectral_index, channel_index, slot_pair, observed):
    comp_count = lax.axis_size("comp")
    group_count = lax.axis_size("freq")
    stations = station_uvw.shape[1]
    side_len = stations // NB
    chans = channel_index.shape[0]
    own_pairs = observed.shape[1]
    per_block = directions.shape[1]
    total_comps = per_block * comp_count
    channels_all = chans * group_count
    scale = 1.0 / math.sqrt(total_comps)
    row_block, col_block = slot_blocks(slot_pair, NB)
    first_slot = lax.axis_index("comp") * own_pairs
    own_rows = lax.dynamic_slice_in_dim(row_block, first_slot, own_pairs)
    own_cols = lax.dynamic_slice_in_dim(col_block, first_slot, own_pairs)
    own_diag = own_rows == own_cols
    ratios = 1.0 + channel_index.astype(jnp.float32) / 4096.0
    phase_list = []
    partial_list = []
    for channel in range(chans):
        phase_re, phase_im = phasor_pair(station_uvw, directions, ratios[channel])
        spectrum = flux_ref * ratios[channel] ** spectral_index * scale
        weighted_re = (spectrum * phase_re.astype(jnp.float32)).astype(jnp.bfloat16)
        weighted_im = (spectrum * phase_im.astype(jnp.float32)).astype(jnp.bfloat16)
        model_re, model_im = model_matrix(weighted_re, weighted_im, phase_re, phase_im)
        block_re = pick_blocks(model_re, row_block, col_block, NB, side_len)
        block_im = pick_blocks(model_im, row_block, col_block, NB, side_len)
        flat_shape = block_re.shape[:-2] + (side_len * side_len,)
        partial_list.append(
            jnp.concatenate([block_re.reshape(flat_shape), block_im.reshape(flat_shape)], axis=-1)
        )
        phase_list.append((phase_re, phase_im))
    partials = jnp.stack(partial_list, axis=0)
    summed = lax.psum_scatter(partials, "comp", scatter_dimension=1, tiled=True)
    summed = summed.reshape(chans, own_pairs, 2, side_len, side_len)
    residual = residual_blocks(summed[:, :, 0], summed[:, :, 1], observed, own_diag, side_len)
    gathered = lax.all_gather(residual, "comp", axis=1, tiled=True)
    matrix_re, matrix_im = hermitian_matrix(gathered, slot_pair, NB, side_len)
    matrix_re = matrix_re.astype(jnp.bfloat16)
    matrix_im = matrix_im.astype(jnp.bfloat16)
    grad_local = jnp.zeros((per_block,), jnp.float32)
    for channel in range(chans):
        terms = contract(
            matrix_re[channel], matrix_im[channel], phase_list[channel][0], phase_list[channel][1]
        )
        grad_local = grad_local + terms * ratios[channel] ** spectral_index
    grad_local = grad_local / (stations * channels_all)
    flux_grad = lax.psum(grad_local, "freq")
    return (residual, flux_grad)


def solution(mesh):
    in_specs = (P(), P(None, "comp"), P("comp"), P("comp"), P("freq"), P(), P("freq", "comp", None))
    out_specs = (P("freq", "comp", None), P("comp"))
    return jax.shard_map(body, mesh=mesh, in_specs=in_specs, out_specs=out_specs, check_vma=False)
```

profile of v0, /device:TPU:1, one launch (start us, length us, event | category | flops | bytes accessed | tf_op | source)
XLA Modules:
  0.0 571.3 jit_solution(3602782162045900699)
XLA Ops:
  7.2 0.8 fusion.82
  8.0 0.8 fusion.81
  8.8 0.7 multiply_add_fusion.2
  9.5 0.6 fusion.83
  11.3 2.0 multiply_multiply_fusion.1
  13.3 4.8 fusion.75
  18.1 5.3 multiply_convert_fusion.3
  23.4 0.7 copy-done.7
  24.2 0.7 fusion.32
  25.0 0.2 fusion.79
  25.2 5.0 reshape.118
  30.2 14.2 %copy.129 = f32[32,32,16,16]{3,2,1,0:T(8,128)} copy(f32[32,32,16,16]{3,1,2,0:T(8,128)} %bitcast.110) | data formatting | bytes 2097152 | tf_op jit(solution)/shard_map/reshape | solution.py:62
  44.5 0.6 select_reduce_fusion.1
  45.1 6.4 %gather_fusion.1 = f32[528,16,16]{2,1,0:T(8,128)} fusion(f32[1024,16,16]{2,1,0:T(8,128)} %bitcast.114, s32[1024]{0:T(1024)S(1)} %pad_clamp_fusion), kind=kCustom, calls=%fused_computation.1 | custom fusion | bytes 1083456 | tf_op jit(solution)/shard_map/gather | solution.py:63
  51.5 3.0 copy.103
  54.5 5.1 reshape.115
  59.6 14.2 %copy.128 = f32[32,32,16,16]{3,2,1,0:T(8,128)} copy(f32[32,32,16,16]{3,1,2,0:T(8,128)} %bitcast.111) | data formatting | bytes 2097152 | tf_op jit(solution)/shard_map/reshape | solution.py:62
  73.8 6.4 %gather_fusion = f32[528,16,16]{2,1,0:T(8,128)} fusion(f32[1024,16,16]{2,1,0:T(8,128)} %bitcast.116, s32[1024]{0:T(1024)S(1)} %pad_clamp_fusion), kind=kCustom, calls=%fused_computation | custom fusion | bytes 1083456 | tf_op jit(solution)/shard_map/gather | solution.py:63
  80.2 3.1 copy.100
  83.4 0.7 fusion.40
  84.2 0.2 fusion.80
  84.3 5.3 reshape.124
  89.6 14.2 %copy.131 = f32[32,32,16,16]{3,2,1,0:T(8,128)} copy(f32[32,32,16,16]{3,1,2,0:T(8,128)} %bitcast.112) | data formatting | bytes 2097152 | tf_op jit(solution)/shard_map/reshape | solution.py:62
  103.8 6.4 %gather_fusion.3 = f32[528,16,16]{2,1,0:T(8,128)} fusion(f32[1024,16,16]{2,1,0:T(8,128)} %bitcast.117, s32[1024]{0:T(1024)S(1)} %pad_clamp_fusion), kind=kCustom, calls=%fused_computation.3 | custom fusion | bytes 1083456 | tf_op jit(solution)/shard_map/gather | solution.py:63
  110.2 3.0 copy.109
  113.3 5.0 reshape.121
  118.3 14.2 %copy.130 = f32[32,32,16,16]{3,2,1,0:T(8,128)} copy(f32[32,32,16,16]{3,1,2,0:T(8,128)} %bitcast.113) | data formatting | bytes 2097152 | tf_op jit(solution)/shard_map/reshape | solution.py:62
  132.5 6.4 %gather_fusion.2 = f32[528,16,16]{2,1,0:T(8,128)} fusion(f32[1024,16,16]{2,1,0:T(8,128)} %bitcast.115, s32[1024]{0:T(1024)S(1)} %pad_clamp_fusion), kind=kCustom, calls=%fused_computation.2 | custom fusion | bytes 1083456 | tf_op jit(solution)/shard_map/gather | solution.py:63
  138.9 3.0 copy.106
  142.3 2.5 copy.110
  145.0 0.2 copy.113
  145.2 0.3 copy-done.24
  145.5 0.6 dynamic-slice
  147.1 173.4 %all-reduce.3.cloned.1.call-done = f32[2,528,512]{2,0,1:T(2,128)} async-done(((f32[2,528,512]{2,0,1:T(2,128)}), f32[2,528,512]{2,0,1:T(2,128)}) %all-reduce.3.cloned.1.call-update) | async-done | bytes 2162704
  320.5 0.9 constant_dynamic-slice_fusion
  321.4 0.2 copy.111
  321.6 0.2 fusion.65
  322.1 0.7 pad_maximum_fusion.1
  322.9 67.5 %all-gather.2.cloned.1.call-done = f32[2,528,512]{2,0,1:T(2,128)} async-done(((f32[2,33,512]{2,0,1:T(2,128)}), f32[2,528,512]{2,0,1:T(2,128)}) %all-gather.2.cloned.1.call-update) | async-done | bytes 2162704 | tf_op jit(solution)/shard_map/all_gather | solution.py:148
  390.4 0.6 broadcast_in_dim.98
  391.0 34.5 %scatter_fusion = f32[2,528,512]{2,0,1:T(2,128)S(1)} fusion(f32[2,528,512]{2,0,1:T(2,128)S(1)} %broadcast_in_dim.98, s32[528]{0:T(1024)S(1)} %compare_select_fusion.1, f32[528,2,512]{2,1,0:T(2,128)} %bitcast.125), kind=kCustom, calls=%fused_computation.5 | custom fusion | bytes 6490176 | tf_op jit(solution)/shard_map/scatter | solution.py:86
  425.5 11.6 %gather_fusion.4 = f32[1024,2,512]{2,1,0:T(2,128)} fusion(f32[2,528,512]{2,0,1:T(2,128)S(1)} %scatter_fusion, s32[1024]{0:T(1024)S(1)} %broadcast_clamp_fusion), kind=kCustom, calls=%fused_computation.4 | custom fusion | bytes 8392704 | tf_op jit(solution)/shard_map/gather | solution.py:87
  437.0 7.3 %copy.120 = f32[2,1024,512]{1,2,0:T(8,128)} copy(f32[2,1024,512]{2,0,1:T(2,128)} %bitcast.118) | data formatting | bytes 8388608 | tf_op jit(solution)/shard_map/gather | solution.py:87
  444.3 11.6 %reshape.131 = f32[2,32,32,2,16,16]{2,1,5,4,3,0:T(8,128)} reshape(f32[2,1024,512]{1,2,0:T(8,128)} %copy.120) | data formatting | bytes 8388608 | tf_op jit(solution)/shard_map/reshape | solution.py:88
  455.9 9.4 %slice_bitcast_fusion = f32[2,32,32,16,16]{2,1,4,3,0:T(8,128)} fusion(f32[2,32,32,2,16,16]{2,1,5,4,3,0:T(8,128)} %reshape.131), kind=kLoop, calls=%fused_computation.6 | loop fusion | bytes 4194304 | tf_op jit(solution)/shard_map/squeeze | solution.py:93
  465.3 1.8 copy-done
  467.1 2.2 fusion.3
  469.3 2.4 fusion.78
  471.7 5.0 copy.126
  476.7 8.4 %squeeze.58 = bf16[512,512]{1,0:T(8,128)(2,1)} reshape(bf16[1,32,16,32,16]{4,3,2,1,0:T(8,128)(2,1)} %copy.126) | data formatting | bytes 1048576 | tf_op jit(solution)/shard_map/squeeze | solution.py:155
  485.1 7.9 %fusion.2 = bf16[2,32,16,32,16]{3,1,4,2,0:T(8,128)(2,1)S(1)} fusion(f32[2,32,32,16,16]{2,1,4,3,0:T(8,128)} %slice_bitcast_fusion, pred[32,32]{1,0:T(8,128)(4,1)S(1)} %bitcast.136), kind=kLoop, calls=%fused_computation.13 | loop fusion | flops 1572864 | bytes 3146752 | tf_op jit(solution)/shard_map/convert_element_type | solution.py:151
  493.0 3.0 fusion.77
  496.1 5.0 copy.127
  501.0 8.0 %squeeze.59 = bf16[512,512]{1,0:T(8,128)(2,1)S(1)} reshape(bf16[1,32,16,32,16]{4,3,2,1,0:T(8,128)(2,1)} %copy.127) | data formatting | bytes 1048576 | tf_op jit(solution)/shard_map/squeeze | solution.py:155
  509.1 1.0 neg.31
  510.0 3.6 copy.123
  513.6 7.9 %squeeze.55 = bf16[512,512]{1,0:T(8,128)(2,1)S(1)} reshape(bf16[1,32,16,32,16]{4,3,2,1,0:T(8,128)(2,1)} %copy.123) | data formatting | bytes 1048576 | tf_op jit(solution)/shard_map/squeeze | solution.py:155
  521.6 3.6 copy.125
  525.2 7.9 %squeeze.57 = bf16[512,512]{1,0:T(8,128)(2,1)S(1)} reshape(bf16[1,32,16,32,16]{4,3,2,1,0:T(8,128)(2,1)} %copy.125) | data formatting | bytes 1048576 | tf_op jit(solution)/shard_map/squeeze | solution.py:155
  533.3 0.7 fusion.29
  534.1 0.2 copy-done.8
  534.3 0.7 fusion.26
  535.1 1.3 add_multiply_fusion
  536.4 27.8 %psum.7 = f32[256]{0:T(256)} all-reduce(f32[256]{0:T(256)S(1)} %add_multiply_fusion), channel_id=1, replica_groups=mesh['comp'=16,'freq'=16] {'freq'}, use_global_device_ids=true, to_apply=%region_6.7 | all-reduce | flops 256 | bytes 2048 | tf_op jit(solution)/shard_map/psum | solution.py:159
  (65 shorter events, 1.4 us)
Async XLA Ops:
  7.2 313.3 %all-reduce.3.cloned.1.call-start = ((), (), s32[]{:S(2)}) async-start(), calls=%async_computation.1 | async-start | bytes 4325376
  23.4 0.7 copy-start.7
  23.4 0.8 copy-start.9
  30.2 14.3 %copy-start.19 = (s32[528]{0:T(1024)S(1)}, s32[528]{0:T(1024)}, u32[]{:S(2)}) copy-start(s32[528]{0:T(1024)} %param.16) | copy-start | bytes 6340
  30.2 14.2 %copy-start.20 = (s32[528]{0:T(1024)S(1)}, s32[528]{0:T(1024)}, u32[]{:S(2)}) copy-start(s32[528]{0:T(1024)} %constant.45.clone) | copy-start | bytes 6340
  30.2 14.2 %copy-start.21 = (s32[528]{0:T(1024)S(1)}, s32[528]{0:T(1024)}, u32[]{:S(2)}) copy-start(s32[528]{0:T(1024)} %constant.46.clone) | copy-start | bytes 6340
  80.2 3.2 copy-start.6
  80.2 3.2 copy-start.11
  80.2 3.2 copy-start.13
  80.2 3.2 copy-start.15
  80.2 3.2 copy-start.16
  142.3 2.6 copy-start.17
  144.9 0.7 copy-start.24
  144.9 245.5 %all-gather.2.cloned.1.call-start = ((), (), s32[]{:S(2)}) async-start(), calls=%async_computation | async-start | bytes 2297856 | tf_op jit(solution)/shard_map/all_gather | solution.py:148
  146.9 176.1 %copy-start.23 = (s32[1024]{0:T(1024)S(1)}, s32[1024]{0:T(1024)}, u32[]{:S(2)}) copy-start(s32[1024]{0:T(1024)} %constant.55) | copy-start | bytes 12292
  444.3 21.0 %copy-start.18 = (pred[32,32]{1,0:T(32,128)(4,1)S(1)}, pred[32,32]{1,0:T(32,128)(4,1)}, u32[]{:S(2)}) copy-start(pred[32,32]{1,0:T(32,128)(4,1)} %constant.48.clone) | copy-start | bytes 3076
  455.9 11.2 %copy-start = (f32[2,32,32,2,16,16]{2,1,5,4,3,0:T(8,128)S(1)}, f32[2,32,32,2,16,16]{2,1,5,4,3,0:T(8,128)}, u32[]{:S(2)}) copy-start(f32[2,32,32,2,16,16]{2,1,5,4,3,0:T(8,128)} %reshape.131) | copy-start | bytes 12582916
  509.1 1.0 copy-start.2
  513.6 7.9 %copy-start.1 = (bf16[1,32,16,32,16]{3,1,4,2,0:T(8,128)(2,1)S(1)}, bf16[1,32,16,32,16]{3,1,4,2,0:T(8,128)(2,1)}, u32[]{:S(2)}) copy-start(bf16[1,32,16,32,16]{3,1,4,2,0:T(8,128)(2,1)} %get-tuple-element.8) | copy-start | bytes 1572868
  525.2 8.1 %copy-start.3 = (bf16[512,512]{1,0:T(8,128)(2,1)S(1)}, bf16[512,512]{1,0:T(8,128)(2,1)}, u32[]{:S(2)}) copy-start(bf16[512,512]{1,0:T(8,128)(2,1)} %copy-done.2) | copy-start | bytes 1572868
  525.2 8.1 %copy-start.4 = (bf16[512,512]{1,0:T(8,128)(2,1)S(1)}, bf16[512,512]{1,0:T(8,128)(2,1)}, u32[]{:S(2)}) copy-start(bf16[512,512]{1,0:T(8,128)(2,1)} %squeeze.58) | copy-start | bytes 1572868
  525.2 8.1 %copy-start.5 = (bf16[512,512]{1,0:T(8,128)(2,1)S(1)}, bf16[512,512]{1,0:T(8,128)(2,1)}, u32[]{:S(2)}) copy-start(bf16[512,512]{1,0:T(8,128)(2,1)} %neg.31) | copy-start | bytes 1572868
  525.2 8.1 %copy-start.12 = (bf16[512,256]{1,0:T(8,128)(2,1)S(1)}, bf16[512,256]{1,0:T(8,128)(2,1)}, u32[]{:S(2)}) copy-start(bf16[512,256]{1,0:T(8,128)(2,1)} %get-tuple-element.30) | copy-start | bytes 786436
  525.2 8.1 %copy-start.14 = (bf16[512,256]{1,0:T(8,128)(2,1)S(1)}, bf16[512,256]{1,0:T(8,128)(2,1)}, u32[]{:S(2)}) copy-start(bf16[512,256]{1,0:T(8,128)(2,1)} %get-tuple-element.31) | copy-start | bytes 786436
  533.3 1.0 copy-start.8
  533.3 1.0 copy-start.10
  534.3 0.7 copy-start.22
Sparse Core Ops, SparseCore 0:
  145.0 175.4 all-reduce.2
  323.9 66.5 all-gather.1
where the time goes:
time: 578 us; the launch traced here: 571 us
  local copies, waits for them, and re-layouts  255 us (44%)
  waiting for transfers between devices  241 us (42%)
  other arithmetic  28.2 us (5%)
  blocking collectives  27.8 us (5%)
  between operations  16.7 us (3%)
    unnamed x3, waiting for transfers between devices  173 us
    all_gather x1, waiting for transfers between devices, body(): gathered = lax.all_gather(residual, 'comp', axis=1, tiled=True)  67.5 us
    reshape x4, local copies, waits for them, and re-layouts, pick_blocks(): block_grid = block_grid.reshape(blocks * blocks, side_len, side_len)  56.8 us
    gather x8, local copies, waits for them, and re-layouts, pick_blocks(): return block_grid[row_block * blocks + col_block]  37.9 us
    scatter x1, local copies, waits for them, and re-layouts, hermitian_matrix(): canonical = jnp.zeros_like(slot_rows).at[:, slot_pair].set(slot_rows)  34.5 us
    psum x1, blocking collectives, body(): flux_grad = lax.psum(grad_local, 'freq')  27.8 us
    reshape x4, local copies, waits for them, and re-layouts, pick_blocks(): matrix.reshape(blocks, side_len, blocks, side_len).transpose(0, 2, 1, 3)  20.4 us
    gather x2, local copies, waits for them, and re-layouts, hermitian_matrix(): arranged = canonical[:, jnp.asarray(grid.reshape(-1))]  18.8 us
  transfers between devices with their start and end apart: 2, of which 2 were waited for; matrix products, arithmetic and copies ran while one was open for 0% of the time, Pallas kernels for 0%

commit v1 on v0

v1 whole, which is shorter than its diff:
```python
import math

import jax
import jax.numpy as jnp
import numpy as np
from jax import lax
from jax.experimental import pallas as pl
from jax.experimental.pallas import tpu as pltpu
from jax.sharding import PartitionSpec as P

NB = 32
GROUP = 8
CHUNK = 256
MAGIC = 12582912.0
SIN_COEF = tuple(
    k * (1.0 - 2.0e-6) for k in (3.14158202, -5.16714276, 2.54189867, -0.55463514)
)


def split3(x):
    hi = lax.reduce_precision(x, 8, 7)
    rest = x - hi
    mid = lax.reduce_precision(rest, 8, 7)
    low = lax.reduce_precision(rest - mid, 8, 7)
    return hi, mid, low


def kernel(ib_ref, jb_ref, lhs_ref, d_ref, ref_ref, res_ref, grad_ref, q_ref, p_ref, g_ref):
    chans = lhs_ref.shape[0]
    comps = d_ref.shape[1]
    slots = ib_ref.shape[0]
    side = 16
    two = 2 * side
    groups = [(g, min(GROUP, slots - g)) for g in range(0, slots, GROUP)]
    width = GROUP * two

    def stack(ref, first, count, cols):
        return jnp.concatenate(
            [q_ref[ref[first + k], :, cols] for k in range(count)], axis=0
        )

    for ch in range(chans):

        @pl.loop(0, comps // CHUNK)
        def _(c):
            cols = pl.ds(pl.multiple_of(c * CHUNK, CHUNK), CHUNK)
            d = d_ref[:, cols]
            hi = d.astype(jnp.bfloat16).astype(jnp.float32)
            rest = d - hi
            mid = rest.astype(jnp.bfloat16).astype(jnp.float32)
            low = (rest - mid).astype(jnp.bfloat16).astype(jnp.float32)
            rhs = jnp.concatenate([hi, mid, low, hi, mid, hi], axis=0).astype(jnp.bfloat16)
            gain = d[3 + ch : 4 + ch]
            root = jnp.sqrt(2.0 * gain)
            coef = [jnp.broadcast_to(-k * root, (8, CHUNK))[None] for k in SIN_COEF]
            gain1 = jnp.broadcast_to(gain, (8, CHUNK))[None]
            gain2 = 2.0 * gain1
            rows = 64
            for r in range(0, lhs_ref.shape[1], rows):
                t = jnp.dot(
                    lhs_ref[ch, r : r + rows], rhs, preferred_element_type=jnp.float32
                ).reshape(rows // 8, 8, CHUNK)
                x = t - ((t + MAGIC) - MAGIC)
                z = x * x
                s = x * (coef[0] + z * (coef[1] + z * (coef[2] + z * coef[3])))
                y = s * s
                w = gain2 - y
                co = w * lax.rsqrt(w)
                im = (s * co).astype(jnp.bfloat16).reshape(rows // side, side, CHUNK)
                re = (gain1 - y).astype(jnp.bfloat16).reshape(rows // side, side, CHUNK)
                b = r // side
                q_ref[b : b + rows // side, 0:side, cols] = re
                q_ref[b : b + rows // side, side:two, cols] = im

        for gi, (first, count) in enumerate(groups):
            size = count * two
            kc = 512
            p_ref[0:size, 0:size] = jnp.zeros((size, size), jnp.float32)

            @pl.loop(0, comps // kc)
            def _(c):
                cols = pl.ds(pl.multiple_of(c * kc, kc), kc)
                a = stack(ib_ref, first, count, cols)
                b = stack(jb_ref, first, count, cols)
                p_ref[0:size, 0:size] += lax.dot_general(
                    a, b, (((1,), (1,)), ((), ())), preferred_element_type=jnp.float32
                )

            lane = lax.broadcasted_iota(jnp.int32, (two, 128), 1)
            row = lax.broadcasted_iota(jnp.int32, (two, 128), 0)
            top = row < side
            for k in range(count):
                base = k * two
                blk = p_ref[base : base + two, (base // 128) * 128 : (base // 128) * 128 + 128]
                if base % 128:
                    blk = pltpu.roll(blk, 128 - base % 128, 1)
                swap = jnp.concatenate([blk[side:], blk[:side]], axis=0)
                swap = pltpu.roll(swap, 128 - side, 1)
                model = blk + jnp.where(top, swap, -swap)
                diag = ib_ref[first + k] == jb_ref[first + k]
                mod_row = jnp.where(top, row, row - side)
                res = model[:, :side] - ref_ref[ch, first + k]
                zero = (mod_row[:, :side] == lane[:, :side]) & diag
                res = jnp.where(zero, 0.0, res)
                res_ref[ch, first + k] = res
                scaled = res * jnp.where(diag, 1.0, 2.0)
                other = jnp.concatenate([-scaled[side:], scaled[:side]], axis=0)
                full = jnp.concatenate([scaled, other], axis=1)
                pieces = [jnp.zeros((two, two * k), jnp.float32)] if k else []
                pieces.append(full)
                if k < count - 1:
                    pieces.append(jnp.zeros((two, two * (count - 1 - k)), jnp.float32))
                line = jnp.concatenate(pieces, axis=1) if len(pieces) > 1 else full
                g_ref[gi, base : base + two, 0:size] = line.astype(jnp.bfloat16)

        @pl.loop(0, comps // CHUNK)
        def _(c):
            cols = pl.ds(pl.multiple_of(c * CHUNK, CHUNK), CHUNK)
            acc = jnp.zeros((8, CHUNK), jnp.float32)
            for gi, (first, count) in enumerate(groups):
                size = count * two
                a = stack(ib_ref, first, count, cols)
                b = stack(jb_ref, first, count, cols)
                m = jnp.dot(g_ref[gi, 0:size, 0:size], b, preferred_element_type=jnp.float32)
                prod = a.astype(jnp.float32) * m
                acc = acc + jnp.sum(prod.reshape(size // 8, 8, CHUNK), axis=0)
            if ch == 0:
                grad_ref[:, cols] = acc
            else:
                grad_ref[:, cols] += acc


def device_kernel(ib, jb, lhs, d, ref):
    chans, stations, _ = lhs.shape
    comps = d.shape[1]
    slots = ref.shape[1]
    vm = pl.BlockSpec(memory_space=pltpu.VMEM)
    sm = pl.BlockSpec(memory_space=pltpu.SMEM)
    width = GROUP * 32
    ngroup = -(-slots // GROUP)
    return pl.pallas_call(
        kernel,
        out_shape=(
            jax.ShapeDtypeStruct(ref.shape, jnp.float32),
            jax.ShapeDtypeStruct((8, comps), jnp.float32),
        ),
        in_specs=[sm, sm, vm, vm, vm],
        out_specs=(vm, vm),
        scratch_shapes=[
            pltpu.VMEM((NB, 32, comps), jnp.bfloat16),
            pltpu.VMEM((width, width), jnp.float32),
            pltpu.VMEM((ngroup, width, width), jnp.bfloat16),
        ],
        compiler_params=pltpu.CompilerParams(vmem_limit_bytes=40 * 2**20),
        name="visibility",
    )(ib, jb, lhs, d, ref)


def station_factors(station_uvw, ratios):
    scaled = ratios[:, None, None] * station_uvw.T[None]
    hi, mid, low = split3(jnp.pad(scaled, ((0, 0), (0, 0), (0, 5))))
    return jnp.concatenate([hi, hi, hi, mid, mid, low], axis=-1).astype(jnp.bfloat16)


def component_rows(directions, flux_ref, spectral_index, ratios, scale):
    l_part = directions[0]
    m_part = directions[1]
    w_term = jnp.sqrt(1.0 - l_part * l_part - m_part * m_part) - 1.0
    gains = [
        jnp.sqrt(flux_ref * ratios[k] ** spectral_index * scale) for k in range(ratios.shape[0])
    ]
    rows = [l_part, m_part, w_term] + gains
    rows += [jnp.zeros_like(l_part)] * (8 - len(rows))
    return jnp.stack(rows, axis=0)


def slot_tables(own_pairs):
    starts = np.asarray([i * NB - i * (i - 1) // 2 for i in range(NB)], np.int32)
    row = jnp.sum((own_pairs[:, None] >= jnp.asarray(starts)[None, :]).astype(jnp.int32), axis=1) - 1
    col = own_pairs - (row * NB - row * (row - 1) // 2) + row
    return row, col


def reference_blocks(observed, on_diag, side):
    chans, slots, _ = observed.shape
    shaped = observed.reshape(chans, slots, 2, side, side)
    above = jnp.asarray(np.arange(side)[:, None] < np.arange(side)[None, :])
    part = jnp.where(above, shaped, 0.0)
    turned = jnp.swapaxes(part, -1, -2)
    herm = jnp.stack([part[:, :, 0] + turned[:, :, 0], part[:, :, 1] - turned[:, :, 1]], axis=2)
    out = jnp.where(on_diag[None, :, None, None, None], herm, shaped)
    return out.reshape(chans, slots, 2 * side, side)


def swap_perm(count, k):
    return [(i, i ^ k) for i in range(count)]


def gather_components(own, count):
    me = lax.axis_index("comp")
    parts = {0: own}
    for k in (1, 2, 3):
        parts[k] = lax.ppermute(own, "comp", swap_perm(count, k))
    low = jnp.stack([parts[k] for k in range(4)], axis=0)
    rounds = {0: low}
    for k in (4, 8, 12):
        rounds[k] = lax.ppermute(low, "comp", swap_perm(count, k))
    return jnp.stack([rounds[k] for k in (0, 4, 8, 12)], axis=0)


def body(station_uvw, directions, flux_ref, spectral_index, channel_index, slot_pair, observed):
    comp_count = lax.axis_size("comp")
    group_count = lax.axis_size("freq")
    stations = station_uvw.shape[1]
    side = stations // NB
    chans = channel_index.shape[0]
    own_slots = observed.shape[1]
    per_block = directions.shape[1]
    total = per_block * comp_count
    scale = 1.0 / math.sqrt(total)
    me = lax.axis_index("comp")
    ratios = 1.0 + channel_index.astype(jnp.float32) / 4096.0

    own = component_rows(directions, flux_ref, spectral_index, ratios, scale)
    d = gather_components(own, comp_count)
    d = d.reshape(comp_count, 8, per_block).transpose(1, 0, 2).reshape(8, total)

    own_pairs = lax.dynamic_slice_in_dim(slot_pair, me * own_slots, own_slots)
    ib, jb = slot_tables(own_pairs)
    ref = reference_blocks(observed, ib == jb, side)
    lhs = station_factors(station_uvw, ratios)
    res, grad = device_kernel(ib, jb, lhs, d, ref)
    residual = res.reshape(chans, own_slots, 2 * side * side)

    part = jnp.sum(grad, axis=0).reshape(comp_count, per_block)
    order = me ^ jnp.arange(comp_count)
    part = part[order]
    sent = jnp.broadcast_to(part[:, None, :], (comp_count, group_count, per_block))
    sent = sent.reshape(comp_count * group_count, per_block)
    got = lax.all_to_all(sent, ("comp", "freq"), 0, 0, tiled=True)
    flux_grad = jnp.sum(got, axis=0) / (flux_ref * (scale * stations * chans * group_count))
    return residual, flux_grad


def solution(mesh):
    in_specs = (P(), P(None, "comp"), P("comp"), P("comp"), P("freq"), P(), P("freq", "comp", None))
    out_specs = (P("freq", "comp", None), P("comp"))
    return jax.shard_map(body, mesh=mesh, in_specs=in_specs, out_specs=out_specs, check_vma=False)
```

time: 578 us -> 109 us (0.19); the launches traced: 571 us -> 108 us
  local copies, waits for them, and re-layouts: 255 us -> 8.59 us
  waiting for transfers between devices: 241 us -> 17.6 us
  Pallas kernels: 0 us -> 47.9 us
  blocking collectives: 27.8 us -> 0 us
  starting transfers between devices: 0.08 us -> 25.3 us
  other arithmetic: 28.2 us -> 7.76 us
  between operations: 16.7 us -> 0.85 us
    unnamed x3 -> x0, waiting for transfers between devices: 173 us -> none
    reshape x11 -> x2, local copies, waits for them, and re-layouts: 89.1 us -> 0.97 us  [the longest x1 0.97 us: reference_blocks(): shaped = observed.reshape(chans, slots, 2, side, side)]
    all_gather x1 -> x0, waiting for transfers between devices: 67.5 us -> none  [body(): gathered = lax.all_gather(residual, 'comp', axis=1, tiled=True)]
    gather x10 -> x1, local copies, waits for them, and re-layouts: 56.7 us -> 0.58 us  [body(): part = part[order]]
    pallas_call x0 -> x1, Pallas kernels: none -> 47.9 us  [device_kernel(): pl.pallas_call(kernel, out_shape=(jax.ShapeDtypeStruct(ref.shape, jnp.flo...]
    squeeze x5 -> x0, local copies, waits for them, and re-layouts: 41.6 us -> none  [the longest x2 16.3 us: body(): matrix_re[channel]]
    scatter x1 -> x0, local copies, waits for them, and re-layouts: 34.5 us -> none  [hermitian_matrix(): canonical = jnp.zeros_like(slot_rows).at[:, slot_pair].set(slot_rows)]
    psum x1 -> x0, blocking collectives: 27.8 us -> none  [body(): flux_grad = lax.psum(grad_local, 'freq')]
  transfers between devices with their start and end apart: 2 -> 7, of which waited for: 2 -> 3; matrix products, arithmetic and copies ran while one was open for 0% -> 8% of each run, Pallas kernels for 0% -> 0%
where the time goes in v1:
time: 109 us; the launch traced here: 108 us
  Pallas kernels  47.9 us (44%)
  starting transfers between devices  25.3 us (23%)
  waiting for transfers between devices  17.6 us (16%)
  local copies, waits for them, and re-layouts  8.59 us (8%)
  other arithmetic  7.76 us (7%)
    pallas_call x1, Pallas kernels, device_kernel(): pl.pallas_call(kernel, out_shape=(jax.ShapeDtypeStruct(ref.shape, jnp.flo...  47.9 us
    all_to_all x1, waiting for transfers between devices, body(): got = lax.all_to_all(sent, ('comp', 'freq'), 0, 0, tiled=True)  13.9 us
    all_to_all x1, starting transfers between devices, body(): got = lax.all_to_all(sent, ('comp', 'freq'), 0, 0, tiled=True)  12.3 us
    ppermute x3, starting transfers between devices, gather_components(): parts[k] = lax.ppermute(own, 'comp', swap_perm(count, k))  9.02 us
    ppermute x3, starting transfers between devices, gather_components(): rounds[k] = lax.ppermute(low, 'comp', swap_perm(count, k))  4.01 us
    ppermute x3, waiting for transfers between devices, gather_components(): rounds[k] = lax.ppermute(low, 'comp', swap_perm(count, k))  3.78 us
  transfers between devices with their start and end apart: 7, of which 3 were waited for; matrix products, arithmetic and copies ran while one was open for 8% of the time, Pallas kernels for 0%

profile of v1, /device:TPU:1, one launch (start us, length us, event | category | flops | bytes accessed | tf_op | source)
XLA Modules:
  0.0 108.1 jit_solution(5010250557788063161)
XLA Ops:
  0.6 0.7 multiply_add_fusion
  1.3 0.6 fusion.6
  1.9 0.8 sqrt_add_fusion
  2.6 2.0 %multiply_sqrt_fusion = (f32[256]{0:T(256)S(1)}, f32[256]{0:T(256)S(1)}) fusion(f32[256]{0:T(256)} %param.11, f32[256]{0:T(256)} %param.12, f32[]{:T(128)} %bitcast.3, f32[]{:T(128)} %bitcast.1), kind=kLoop, calls=%fused_computation.30 | loop fusion | flops 1024 | bytes 4104 | tf_op jit(solution)/shard_map/sqrt | solution.py:170
  4.7 0.7 stack.54
  5.4 3.9 %collective-permute-start = (f32[8,256]{1,0:T(8,128)S(1)}, f32[8,256]{1,0:T(8,128)S(1)}, u32[]{:S(2)}, u32[]{:S(2)}) collective-permute-start(f32[8,256]{1,0:T(8,128)S(1)} %stack.54), channel_id=1, source_target_pairs={{0,16},{16,0},{32,48},{48,32},{64,80},{80,64},{96,112},{112,96},{1... | collective-permute-start | bytes 24584 | tf_op jit(solution)/shard_map/ppermute | solution.py:203
  9.3 5.1 %collective-permute-start.1 = (f32[8,256]{1,0:T(8,128)S(1)}, f32[8,256]{1,0:T(8,128)S(1)}, u32[]{:S(2)}, u32[]{:S(2)}) collective-permute-start(f32[8,256]{1,0:T(8,128)S(1)} %stack.54), channel_id=1, source_target_pairs={{0,32},{16,48},{32,0},{48,16},{64,96},{80,112},{96,64},{112,80},{1... | collective-permute-start | bytes 24584 | tf_op jit(solution)/shard_map/ppermute | solution.py:203
  14.4 0.0 collective-permute-start.2
  14.4 0.8 dynamic_slice.3
  15.2 0.7 convert_reduce_fusion
  15.9 0.8 fusion.4
  16.7 0.8 broadcast_multiply_fusion
  17.5 1.1 %copy.32 = f32[2,33,512]{1,2,0:T(8,128)S(1)} copy(f32[2,33,512]{2,0,1:T(2,128)} %param.15) | data formatting | bytes 270336 | tf_op args[6]
  18.7 0.8 broadcast_select_fusion
  19.5 0.2 copy.41
  19.6 0.1 slice_add_fusion
  19.7 1.0 copy.34
  20.7 1.0 copy.36
  21.7 0.2 bitcast_select_fusion.ref_ref
  21.9 0.0 collective-permute-done
  21.9 0.0 collective-permute-done.1
  21.9 0.0 collective-permute-done.2
  21.9 1.4 %collective-permute-start.3 = (f32[4,8,256]{2,1,0:T(8,128)S(1)}, f32[4,8,256]{2,1,0:T(8,128)S(1)}, u32[]{:S(2)}, u32[]{:S(2)}) collective-permute-start(f32[4,8,256]{2,1,0:T(8,128)S(1)} %get-tuple-element.19), channel_id=1, source_target_pairs={{0,64},{16,80},{32,96},{48,112},{64,0},{80,16},{96,32},{112,48},{1... | collective-permute-start | bytes 98312 | tf_op jit(solution)/shard_map/ppermute | solution.py:207
  23.3 2.6 %collective-permute-start.4 = (f32[4,8,256]{2,1,0:T(8,128)S(1)}, f32[4,8,256]{2,1,0:T(8,128)S(1)}, u32[]{:S(2)}, u32[]{:S(2)}) collective-permute-start(f32[4,8,256]{2,1,0:T(8,128)S(1)} %get-tuple-element.19), channel_id=1, source_target_pairs={{0,128},{16,144},{32,160},{48,176},{64,192},{80,208},{96,224},{112... | collective-permute-start | bytes 98312 | tf_op jit(solution)/shard_map/ppermute | solution.py:207
  25.9 0.0 collective-permute-start.5
  25.9 0.2 copy.37.lhs_ref
  26.1 0.0 collective-permute-done.3
  26.1 1.5 %collective-permute-done.4 = f32[4,8,256]{2,1,0:T(8,128)S(1)} collective-permute-done((f32[4,8,256]{2,1,0:T(8,128)S(1)}, f32[4,8,256]{2,1,0:T(8,128)S(1)}, u32[]{:S(2)}, u32[]{:S(2)}) %collective-permute-start.4) | collective-permute-done | bytes 32800 | tf_op jit(solution)/shard_map/ppermute | solution.py:207
  27.6 2.3 %collective-permute-done.5 = f32[4,8,256]{2,1,0:T(8,128)S(1)} collective-permute-done((f32[4,8,256]{2,1,0:T(8,128)S(1)}, f32[4,8,256]{2,1,0:T(8,128)S(1)}, u32[]{:S(2)}, u32[]{:S(2)}) %collective-permute-start.5) | collective-permute-done | bytes 32800 | tf_op jit(solution)/shard_map/ppermute | solution.py:207
  29.9 47.9 %visibility.1 = (f32[2,33,32,16]{3,2,1,0:T(8,128)S(1)}, f32[8,4096]{1,0:T(8,128)S(1)}) custom-call(s32[33]{0:T(128)S(1)} %broadcast_add_fusion.ib_ref, s32[33]{0:T(128)S(1)} %get-tuple-element.15.jb_ref, bf16[2,512,48]{2,1,0:T(8,128)(2,1)S(1)} %copy.37.lhs_ref, f32[8,4096]{1,0:T(8,128)S(1)} %bitcast.29, f32[2,33,32,16]{3,2,1,0:T(8,128)S(1)} %bitcast_select_fusion.ref_ref), custom_call_target="tpu_custom_call" | custom-call | tf_op jit(solution)/shard_map/visibility/pallas_call | solution.py:141
  77.9 0.6 gather_fusion
  78.5 1.0 all_to_all.6
  79.5 12.3 %all-to-all-start = ((f32[256,1,256]{2,1,0:T(1,128)}), f32[256,1,256]{2,1,0:T(1,128)S(1)}, u32[]{:S(2)}, u32[]{:S(2)}) async-start(f32[256,1,256]{2,1,0:T(1,128)} %all_to_all.6), calls=%async_computation | async-start | bytes 524288 | tf_op jit(solution)/shard_map/all_to_all | solution.py:240
  91.8 0.0 copy-start
  91.8 0.7 copy.38
  92.5 0.9 copy.39
  93.4 13.9 %all-to-all-done = f32[256,1,256]{2,1,0:T(1,128)S(1)} async-done(((f32[256,1,256]{2,1,0:T(1,128)}), f32[256,1,256]{2,1,0:T(1,128)S(1)}, u32[]{:S(2)}, u32[]{:S(2)}) %all-to-all-start) | async-done | bytes 262176 | tf_op jit(solution)/shard_map/all_to_all | solution.py:240
  107.2 0.3 reduce_sum.29
  107.5 0.0 copy-done
  107.5 0.6 multiply_divide_fusion
  (17 shorter events, 0.2 us)
Async XLA Ops:
  5.4 16.5 %collective-permute-start = (f32[8,256]{1,0:T(8,128)S(1)}, f32[8,256]{1,0:T(8,128)S(1)}, u32[]{:S(2)}, u32[]{:S(2)}) collective-permute-start(f32[8,256]{1,0:T(8,128)S(1)} %stack.54), channel_id=1, source_target_pairs={{0,16},{16,0},{32,48},{48,32},{64,80},{80,64},{96,112},{112,96},{1... | collective-permute-start | bytes 24584 | tf_op jit(solution)/shard_map/ppermute | solution.py:203
  9.3 12.6 %collective-permute-start.1 = (f32[8,256]{1,0:T(8,128)S(1)}, f32[8,256]{1,0:T(8,128)S(1)}, u32[]{:S(2)}, u32[]{:S(2)}) collective-permute-start(f32[8,256]{1,0:T(8,128)S(1)} %stack.54), channel_id=1, source_target_pairs={{0,32},{16,48},{32,0},{48,16},{64,96},{80,112},{96,64},{112,80},{1... | collective-permute-start | bytes 24584 | tf_op jit(solution)/shard_map/ppermute | solution.py:203
  14.4 7.5 %collective-permute-start.2 = (f32[8,256]{1,0:T(8,128)S(1)}, f32[8,256]{1,0:T(8,128)S(1)}, u32[]{:S(2)}, u32[]{:S(2)}) collective-permute-start(f32[8,256]{1,0:T(8,128)S(1)} %stack.54), channel_id=1, source_target_pairs={{0,48},{16,32},{32,16},{48,0},{64,112},{80,96},{96,80},{112,64},{1... | collective-permute-start | bytes 24584 | tf_op jit(solution)/shard_map/ppermute | solution.py:203
  21.9 4.2 %collective-permute-start.3 = (f32[4,8,256]{2,1,0:T(8,128)S(1)}, f32[4,8,256]{2,1,0:T(8,128)S(1)}, u32[]{:S(2)}, u32[]{:S(2)}) collective-permute-start(f32[4,8,256]{2,1,0:T(8,128)S(1)} %get-tuple-element.19), channel_id=1, source_target_pairs={{0,64},{16,80},{32,96},{48,112},{64,0},{80,16},{96,32},{112,48},{1... | collective-permute-start | bytes 98312 | tf_op jit(solution)/shard_map/ppermute | solution.py:207
  23.3 4.3 %collective-permute-start.4 = (f32[4,8,256]{2,1,0:T(8,128)S(1)}, f32[4,8,256]{2,1,0:T(8,128)S(1)}, u32[]{:S(2)}, u32[]{:S(2)}) collective-permute-start(f32[4,8,256]{2,1,0:T(8,128)S(1)} %get-tuple-element.19), channel_id=1, source_target_pairs={{0,128},{16,144},{32,160},{48,176},{64,192},{80,208},{96,224},{112... | collective-permute-start | bytes 98312 | tf_op jit(solution)/shard_map/ppermute | solution.py:207
  25.9 4.0 %collective-permute-start.5 = (f32[4,8,256]{2,1,0:T(8,128)S(1)}, f32[4,8,256]{2,1,0:T(8,128)S(1)}, u32[]{:S(2)}, u32[]{:S(2)}) collective-permute-start(f32[4,8,256]{2,1,0:T(8,128)S(1)} %get-tuple-element.19), channel_id=1, source_target_pairs={{0,192},{16,208},{32,224},{48,240},{64,128},{80,144},{96,160},{112... | collective-permute-start | bytes 98312 | tf_op jit(solution)/shard_map/ppermute | solution.py:207
  79.5 27.8 %all-to-all-start = ((f32[256,1,256]{2,1,0:T(1,128)}), f32[256,1,256]{2,1,0:T(1,128)S(1)}, u32[]{:S(2)}, u32[]{:S(2)}) async-start(f32[256,1,256]{2,1,0:T(1,128)} %all_to_all.6), calls=%async_computation | async-start | bytes 524288 | tf_op jit(solution)/shard_map/all_to_all | solution.py:240
  91.8 15.7 %copy-start = (f32[256]{0:T(256)S(1)}, f32[256]{0:T(256)}, u32[]{:S(2)}) copy-start(f32[256]{0:T(256)} %param.11) | copy-start | bytes 3076

commit v2 on v1

v2 whole, which is shorter than its diff:
```python
import math

import jax
import jax.numpy as jnp
import numpy as np
from jax import lax
from jax.experimental import pallas as pl
from jax.experimental.pallas import tpu as pltpu
from jax.sharding import PartitionSpec as P

NB = 32
GROUP = 8
CHUNK = 512
ROWS = 64
SIN_COEF = tuple(
    k * (1.0 - 2.0e-6) for k in (3.14158202, -5.16714276, 2.54189867, -0.55463514)
)


def pieces(x):
    hi = x.astype(jnp.bfloat16).astype(jnp.float32)
    rest = x - hi
    mid = rest.astype(jnp.bfloat16).astype(jnp.float32)
    low = (rest - mid).astype(jnp.bfloat16).astype(jnp.float32)
    return hi, mid, low


def kernel(
    ib_ref, jb_ref, dest_ref, ratio_ref, uvw_ref, d_ref, ref_ref, res_ref, sent_ref, lhs_ref, acc_ref, *rest
):
    chans, slots, two, side = ref_ref.shape
    blocks, _, width = d_ref.shape
    stations = uvw_ref.shape[1]
    copies = sent_ref.shape[0] // blocks
    comps = blocks * width
    scale = 1.0 / math.sqrt(comps)
    steps = comps // CHUNK
    per = CHUNK // width
    groups = [(g, min(GROUP, slots - g)) for g in range(0, slots, GROUP)]
    count_g = len(groups)
    p_refs = rest[: chans * count_g]
    g_refs = rest[chans * count_g : 2 * chans * count_g]
    q_refs = rest[2 * chans * count_g :]

    def stack(q_ref, ref, first, count):
        return jnp.concatenate([q_ref[ref[first + k]] for k in range(count)], axis=0)

    def stations_of(ch):
        uvw = jnp.concatenate(
            [uvw_ref[...] * ratio_ref[0, ch], jnp.zeros((5, stations), jnp.float32)], axis=0
        )
        hi, mid, low = pieces(uvw)
        rows = jnp.concatenate([hi, hi, hi, mid, mid, low], axis=0)
        lhs_ref[ch] = rows.T.astype(jnp.bfloat16)

    def phasors(ch, step):
        q_ref = q_refs[ch * steps + step]
        d = jnp.concatenate([d_ref[step * per + k] for k in range(per)], axis=1)
        l_part, m_part = d[0:1], d[1:2]
        w_term = jnp.sqrt(1.0 - l_part * l_part - m_part * m_part) - 1.0
        row = lax.broadcasted_iota(jnp.int32, d.shape, 0)
        hi, mid, low = pieces(jnp.where(row == 2, w_term, d))
        rhs = jnp.concatenate([hi, mid, low, hi, mid, hi], axis=0).astype(jnp.bfloat16)
        gain = jnp.sqrt(d[3:4] * jnp.exp2(d[4:5] * ratio_ref[1, ch]) * scale)
        root = jnp.sqrt(2.0 * gain)
        coef = [jnp.broadcast_to(-k * root, (8, CHUNK))[None] for k in SIN_COEF]
        gain1 = jnp.broadcast_to(gain, (8, CHUNK))[None]
        gain2 = 2.0 * gain1
        for r in range(0, stations, ROWS):
            t = jnp.dot(
                lhs_ref[ch, r : r + ROWS], rhs, preferred_element_type=jnp.float32
            ).reshape(ROWS // 8, 8, CHUNK)
            x = t - jnp.round(t)
            z = x * x
            poly = coef[-1]
            for k in coef[-2::-1]:
                poly = k + z * poly
            s = x * poly
            y = s * s
            w = gain2 - y
            co = w * lax.rsqrt(w)
            im = (s * co).astype(jnp.bfloat16).reshape(ROWS // side, side, CHUNK)
            re = (gain1 - y).astype(jnp.bfloat16).reshape(ROWS // side, side, CHUNK)
            b = r // side
            q_ref[b : b + ROWS // side, 0:side] = re
            q_ref[b : b + ROWS // side, side:two] = im

    def model(ch, step):
        q_ref = q_refs[ch * steps + step]
        for gi, (first, count) in enumerate(groups):
            size = count * two
            part = lax.dot_general(
                stack(q_ref, ib_ref, first, count),
                stack(q_ref, jb_ref, first, count),
                (((1,), (1,)), ((), ())),
                preferred_element_type=jnp.float32,
            )
            p_ref = p_refs[ch * count_g + gi]
            if step == 0:
                p_ref[0:size, 0:size] = part
            else:
                p_ref[0:size, 0:size] += part

    def residuals(ch):
        lane = lax.broadcasted_iota(jnp.int32, (two, 128), 1)
        row = lax.broadcasted_iota(jnp.int32, (two, 128), 0)
        top = row < side
        auto = jnp.where(top, row, row - side) == lane
        pad = jnp.zeros((two, 128 - side), jnp.float32)
        for gi, (first, count) in enumerate(groups):
            p_ref = p_refs[ch * count_g + gi]
            g_ref = g_refs[ch * count_g + gi]
            g_ref[...] = jnp.zeros(g_ref.shape, g_ref.dtype)
            for k in range(count):
                base = k * two
                window = (base // 128) * 128
                shift = base % 128
                blk = p_ref[base : base + two, window : window + 128]
                if shift:
                    blk = pltpu.roll(blk, 128 - shift, 1)
                swap = jnp.concatenate([blk[side:], -blk[:side]], axis=0)
                swap = pltpu.roll(swap, 128 - side, 1)
                diag = ib_ref[first + k] == jb_ref[first + k]
                seen = jnp.concatenate([ref_ref[ch, first + k], pad], axis=1)
                res = blk + swap - seen
                res = jnp.where((lane >= side) | (auto & diag), 0.0, res)
                res_ref[ch, first + k] = res[:, :side]
                scaled = res * jnp.where(diag, 1.0, 2.0)
                other = jnp.concatenate([-scaled[side:], scaled[:side]], axis=0)
                full = scaled + pltpu.roll(other, side, 1)
                if shift:
                    full = pltpu.roll(full, shift, 1)
                g_ref[base : base + two, window : window + 128] = full.astype(jnp.bfloat16)

    def gradient(ch, step):
        q_ref = q_refs[ch * steps + step]
        acc = jnp.zeros((8, CHUNK), jnp.float32)
        for gi, (first, count) in enumerate(groups):
            size = count * two
            m = jnp.dot(
                g_refs[ch * count_g + gi][0:size, 0:size],
                stack(q_ref, jb_ref, first, count),
                preferred_element_type=jnp.float32,
            )
            m = stack(q_ref, ib_ref, first, count).astype(jnp.float32) * m
            acc = acc + jnp.sum(m.reshape(size // 8, 8, CHUNK), axis=0)
        if ch > 0:
            acc = acc + acc_ref[step]
        if ch < chans - 1:
            acc_ref[step] = acc
            return
        total = jnp.sum(acc, axis=0, keepdims=True)
        for k in range(per):
            line = total[:, k * width : (k + 1) * width]
            sent_ref[pl.ds(dest_ref[step * per + k] * copies, copies)] = jnp.broadcast_to(
                line[None], (copies, 1, width)
            )

    for ch in range(chans):
        stations_of(ch)
    for ch in range(chans):
        for step in range(steps):
            phasors(ch, step)
            if step > 0:
                model(ch, step - 1)
                if ch > 0:
                    gradient(ch - 1, step - 1)
            elif ch > 0:
                model(ch - 1, steps - 1)
                residuals(ch - 1)
    last = chans - 1
    model(last, steps - 1)
    if last > 0:
        gradient(last - 1, steps - 1)
    residuals(last)
    for step in range(steps):
        gradient(last, step)


def device_kernel(ib, jb, dest, ratio, uvw, d, ref, copies):
    chans, slots, two, _ = ref.shape
    blocks, _, width = d.shape
    stations = uvw.shape[1]
    steps = blocks * width // CHUNK
    vm = pl.BlockSpec(memory_space=pltpu.VMEM)
    sm = pl.BlockSpec(memory_space=pltpu.SMEM)
    side = GROUP * two
    count = chans * -(-slots // GROUP)
    return pl.pallas_call(
        kernel,
        out_shape=(
            jax.ShapeDtypeStruct(ref.shape, jnp.float32),
            jax.ShapeDtypeStruct((blocks * copies, 1, width), jnp.float32),
        ),
        in_specs=[sm, sm, sm, sm, vm, vm, vm],
        out_specs=(vm, vm),
        scratch_shapes=[
            pltpu.VMEM((chans, stations, 48), jnp.bfloat16),
            pltpu.VMEM((steps, 8, CHUNK), jnp.float32),
        ]
        + [pltpu.VMEM((side, side), jnp.float32)] * count
        + [pltpu.VMEM((side, side), jnp.bfloat16)] * count
        + [pltpu.VMEM((NB, two, CHUNK), jnp.bfloat16)] * (chans * steps),
        compiler_params=pltpu.CompilerParams(vmem_limit_bytes=48 * 2**20),
        name="visibility",
    )(ib, jb, dest, ratio, uvw, d, ref)


def slot_tables(own_pairs):
    starts = np.asarray([i * NB - i * (i - 1) // 2 for i in range(NB)], np.int32)
    row = jnp.sum((own_pairs[:, None] >= jnp.asarray(starts)[None, :]).astype(jnp.int32), axis=1) - 1
    col = own_pairs - (row * NB - row * (row - 1) // 2) + row
    return row, col


def reference_blocks(observed, on_diag, side):
    chans, slots, _ = observed.shape
    shaped = observed.reshape(chans, slots, 2, side, side)
    above = jnp.asarray(np.arange(side)[:, None] < np.arange(side)[None, :])
    part = jnp.where(above, shaped, 0.0)
    turned = jnp.swapaxes(part, -1, -2)
    herm = jnp.stack([part[:, :, 0] + turned[:, :, 0], part[:, :, 1] - turned[:, :, 1]], axis=2)
    out = jnp.where(on_diag[None, :, None, None, None], herm, shaped)
    return out.reshape(chans, slots, 2 * side, side)


def swap_perm(count, k):
    return [(i, i ^ k) for i in range(count)]


def gather_components(own, count):
    me = lax.axis_index("comp")
    parts = {0: own}
    for k in (1, 2, 3):
        parts[k] = lax.ppermute(own, "comp", swap_perm(count, k))
    low = jnp.stack([parts[k] for k in range(4)], axis=0)
    rounds = {0: low}
    for k in (4, 8, 12):
        rounds[k] = lax.ppermute(low, "comp", swap_perm(count, k))
    return jnp.stack([rounds[k] for k in (0, 4, 8, 12)], axis=0)


def body(station_uvw, directions, flux_ref, spectral_index, channel_index, slot_pair, observed):
    comp_count = lax.axis_size("comp")
    group_count = lax.axis_size("freq")
    stations = station_uvw.shape[1]
    side = stations // NB
    chans = channel_index.shape[0]
    own_slots = observed.shape[1]
    per_block = directions.shape[1]
    total = per_block * comp_count
    scale = 1.0 / math.sqrt(total)
    me = lax.axis_index("comp")
    ratios = 1.0 + channel_index.astype(jnp.float32) / 4096.0

    blank = jnp.zeros((3, per_block), jnp.float32)
    own = jnp.concatenate(
        [directions, blank[:1], flux_ref[None], spectral_index[None], blank], axis=0
    )
    d = gather_components(own, comp_count).reshape(comp_count, 8, per_block)
    dest = me ^ jnp.arange(comp_count, dtype=jnp.int32)
    ratio = jnp.stack([ratios, jnp.log2(ratios)], axis=0)

    own_pairs = lax.dynamic_slice_in_dim(slot_pair, me * own_slots, own_slots)
    ib, jb = slot_tables(own_pairs)
    ref = reference_blocks(observed, ib == jb, side)
    res, sent = device_kernel(ib, jb, dest, ratio, station_uvw, d, ref, group_count)
    residual = res.reshape(chans, own_slots, 2 * side * side)
    got = lax.all_to_all(sent, ("comp", "freq"), 0, 0, tiled=True)
    flux_grad = jnp.sum(got, axis=(0, 1)) / (flux_ref * (scale * stations * chans * group_count))
    return residual, flux_grad


def solution(mesh):
    in_specs = (P(), P(None, "comp"), P("comp"), P("comp"), P("freq"), P(), P("freq", "comp", None))
    out_specs = (P("freq", "comp", None), P("comp"))
    return jax.shard_map(body, mesh=mesh, in_specs=in_specs, out_specs=out_specs, check_vma=False)
```

time: 109 us -> 75.1 us (0.69)
  Pallas kernels: 47.9 us -> 20.9 us
  other arithmetic: 7.76 us -> 3.48 us
  local copies, waits for them, and re-layouts: 8.59 us -> 6.29 us
    pallas_call x1, Pallas kernels: 47.9 us -> 20.9 us  [device_kernel(): pl.pallas_call(kernel, out_shape=(jax.ShapeDtypeStruct(ref.shape, jnp.flo...]
    sqrt x1 -> x0, other arithmetic: 2.01 us -> none  [component_rows(): jnp.sqrt(flux_ref * ratios[k] ** spectral_index * scale)]
    all_to_all x1, starting transfers between devices: 12.3 us -> 13.5 us  [body(): got = lax.all_to_all(sent, ('comp', 'freq'), 0, 0, tiled=True)]
  transfers between devices with their start and end apart: 7 -> 7, of which waited for: 3 -> 3; matrix products, arithmetic and copies ran while one was open for 8% -> 11% of each run, Pallas kernels for 0% -> 0%
where the time goes in v2:
time: 75.1 us; the launch traced here: 74.8 us
  starting transfers between devices  26.3 us (35%)
  Pallas kernels  20.9 us (28%)
  waiting for transfers between devices  17.1 us (23%)
  local copies, waits for them, and re-layouts  6.29 us (8%)
  other arithmetic  3.48 us (5%)
  between operations  0.79 us (1%)
    pallas_call x1, Pallas kernels, device_kernel(): pl.pallas_call(kernel, out_shape=(jax.ShapeDtypeStruct(ref.shape, jnp.flo...  20.9 us
    all_to_all x1, waiting for transfers between devices, body(): got = lax.all_to_all(sent, ('comp', 'freq'), 0, 0, tiled=True)  13.9 us
    all_to_all x1, starting transfers between devices, body(): got = lax.all_to_all(sent, ('comp', 'freq'), 0, 0, tiled=True)  13.5 us
    ppermute x3, starting transfers between devices, gather_components(): parts[k] = lax.ppermute(own, 'comp', swap_perm(count, k))  9.02 us
    ppermute x3, starting transfers between devices, gather_components(): rounds[k] = lax.ppermute(low, 'comp', swap_perm(count, k))  3.78 us
    ppermute x3, waiting for transfers between devices, gather_components(): rounds[k] = lax.ppermute(low, 'comp', swap_perm(count, k))  3.2 us
    unnamed x8, local copies, waits for them, and re-layouts  1.99 us
  transfers between devices with their start and end apart: 7, of which 3 were waited for; matrix products, arithmetic and copies ran while one was open for 11% of the time, Pallas kernels for 0%

profile of v2, /device:TPU:1, one launch (start us, length us, event | category | flops | bytes accessed | tf_op | source)
XLA Modules:
  0.0 74.8 jit_solution(11032734952460130692)
XLA Ops:
  0.6 0.7 concatenate.3
  1.4 3.9 %collective-permute-start = (f32[8,256]{1,0:T(8,128)S(1)}, f32[8,256]{1,0:T(8,128)S(1)}, u32[]{:S(2)}, u32[]{:S(2)}) collective-permute-start(f32[8,256]{1,0:T(8,128)S(1)} %concatenate.3), channel_id=1, source_target_pairs={{0,16},{16,0},{32,48},{48,32},{64,80},{80,64},{96,112},{112,96},{1... | collective-permute-start | bytes 24584 | tf_op jit(solution)/shard_map/ppermute | solution.py:235
  5.3 5.1 %collective-permute-start.1 = (f32[8,256]{1,0:T(8,128)S(1)}, f32[8,256]{1,0:T(8,128)S(1)}, u32[]{:S(2)}, u32[]{:S(2)}) collective-permute-start(f32[8,256]{1,0:T(8,128)S(1)} %concatenate.3), channel_id=1, source_target_pairs={{0,32},{16,48},{32,0},{48,16},{64,96},{80,112},{96,64},{112,80},{1... | collective-permute-start | bytes 24584 | tf_op jit(solution)/shard_map/ppermute | solution.py:235
  10.4 0.0 collective-permute-start.2
  10.4 0.8 %dynamic_slice.3 = s32[33]{0:T(128)S(1)} dynamic-slice(s32[528]{0:T(1024)} %param.14, s32[]{:T(128)S(6)} %select_n.17), dynamic_slice_sizes={33} | dynamic-slice | bytes 268 | tf_op jit(solution)/shard_map/dynamic_slice | solution.py:264
  11.2 0.7 convert_reduce_fusion
  11.9 0.8 %fusion.1 = (pred[33]{0:T(512)(128)(4,1)S(1)}, s32[33]{0:T(128)S(1)}) fusion(s32[33]{0:T(128)S(1)} %convert_reduce_fusion, s32[528]{0:T(1024)} %param.14, s32[]{:T(128)S(6)} %select_n.17), kind=kLoop, calls=%fused_computation.21 | loop fusion | flops 759 | bytes 433 | tf_op jit(solution)/shard_map/eq | solution.py:266
  12.7 1.1 %copy.22 = f32[2,33,512]{1,2,0:T(8,128)S(1)} copy(f32[2,33,512]{2,0,1:T(2,128)} %param.15) | data formatting | bytes 270336 | tf_op args[6]
  13.8 0.8 %broadcast_select_fusion = f32[2,33,2,16,16]{1,4,3,2,0:T(8,128)S(1)} fusion(f32[2,33,2,16,16]{1,4,3,2,0:T(8,128)S(1)} %bitcast.25, pred[16,16]{1,0:T(8,128)(4,1)} %constant.49.clone), kind=kLoop, calls=%fused_computation.5 | loop fusion | flops 33792 | bytes 270592 | tf_op jit(solution)/shard_map/jit(_where)/select_n | solution.py:220
  14.6 0.2 copy.30
  14.8 0.1 slice_add_fusion
  14.9 1.0 %copy.24 = f32[2,33,2,16,16]{4,3,2,1,0:T(8,128)S(1)} copy(f32[2,33,2,16,16]{1,4,3,2,0:T(8,128)S(1)} %pad_maximum_fusion) | data formatting | bytes 270336 | tf_op jit(solution)/shard_map/stack | solution.py:222
  15.9 0.0 copy-start.2
  15.9 1.0 %copy.26 = f32[2,33,32,16]{3,2,1,0:T(8,128)S(1)} copy(f32[2,33,32,16]{1,3,2,0:T(8,128)S(1)} %bitcast.26) | data formatting | bytes 270336 | tf_op jit(solution)/shard_map/reshape | solution.py:218
  16.8 0.0 copy-done.2
  16.8 0.0 copy-start
  16.9 0.2 bitcast_select_fusion.ref_ref
  17.0 0.0 collective-permute-done
  17.1 0.0 collective-permute-done.1
  17.1 0.0 collective-permute-done.2
  17.1 3.0 %collective-permute-start.4 = (f32[4,8,256]{2,1,0:T(8,128)S(1)}, f32[4,8,256]{2,1,0:T(8,128)S(1)}, u32[]{:S(2)}, u32[]{:S(2)}) collective-permute-start(f32[4,8,256]{2,1,0:T(8,128)S(1)} %get-tuple-element.17), channel_id=1, source_target_pairs={{0,128},{16,144},{32,160},{48,176},{64,192},{80,208},{96,224},{112... | collective-permute-start | bytes 98312 | tf_op jit(solution)/shard_map/ppermute | solution.py:239
  20.1 0.8 %collective-permute-start.5 = (f32[4,8,256]{2,1,0:T(8,128)S(1)}, f32[4,8,256]{2,1,0:T(8,128)S(1)}, u32[]{:S(2)}, u32[]{:S(2)}) collective-permute-start(f32[4,8,256]{2,1,0:T(8,128)S(1)} %get-tuple-element.17), channel_id=1, source_target_pairs={{0,192},{16,208},{32,224},{48,240},{64,128},{80,144},{96,160},{112... | collective-permute-start | bytes 98312 | tf_op jit(solution)/shard_map/ppermute | solution.py:239
  20.9 0.0 collective-permute-start.3
  20.9 0.6 collective-permute-done.4
  21.5 2.6 %collective-permute-done.5 = f32[4,8,256]{2,1,0:T(8,128)S(1)} collective-permute-done((f32[4,8,256]{2,1,0:T(8,128)S(1)}, f32[4,8,256]{2,1,0:T(8,128)S(1)}, u32[]{:S(2)}, u32[]{:S(2)}) %collective-permute-start.5) | collective-permute-done | bytes 32800 | tf_op jit(solution)/shard_map/ppermute | solution.py:239
  24.1 0.0 collective-permute-done.3
  24.1 0.0 copy-done
  24.1 20.9 %visibility.1 = (f32[2,33,32,16]{3,2,1,0:T(8,128)S(1)}, f32[256,1,256]{2,1,0:T(1,128)}) custom-call(s32[33]{0:T(128)S(1)} %broadcast_add_fusion.ib_ref, s32[33]{0:T(128)S(1)} %get-tuple-element.13.jb_ref, s32[16]{0:T(128)S(1)} %iota_xor_fusion.dest_ref, f32[2,2]{1,0:T(2,128)S(1)} %pad_maximum_fusion.3.ratio_ref, f32[3,512]{1,0:T(4,128)S(1)} %copy-done, ...), custom_call_target="tpu_custom_call" | custom-call | tf_op jit(solution)/shard_map/visibility/pallas_call | solution.py:189
  45.0 13.5 %all-to-all-start = ((f32[256,1,256]{2,1,0:T(1,128)}), f32[256,1,256]{2,1,0:T(1,128)S(1)}, u32[]{:S(2)}, u32[]{:S(2)}) async-start(f32[256,1,256]{2,1,0:T(1,128)} %get-tuple-element.5), calls=%async_computation | async-start | bytes 524288 | tf_op jit(solution)/shard_map/all_to_all | solution.py:269
  58.5 0.0 copy-start.1
  58.5 0.7 copy.27
  59.2 0.9 %copy.28 = f32[2,33,512]{2,0,1:T(2,128)} copy(f32[2,33,512]{1,2,0:T(8,128)S(1)} %bitcast.27) | data formatting | bytes 270336
  60.0 13.9 %all-to-all-done = f32[256,1,256]{2,1,0:T(1,128)S(1)} async-done(((f32[256,1,256]{2,1,0:T(1,128)}), f32[256,1,256]{2,1,0:T(1,128)S(1)}, u32[]{:S(2)}, u32[]{:S(2)}) %all-to-all-start) | async-done | bytes 262176 | tf_op jit(solution)/shard_map/all_to_all | solution.py:269
  73.9 0.3 reduce_sum.19
  74.2 0.0 copy-done.1
  74.2 0.6 multiply_divide_fusion
  (9 shorter events, 0.1 us)
Async XLA Ops:
  1.4 15.7 %collective-permute-start = (f32[8,256]{1,0:T(8,128)S(1)}, f32[8,256]{1,0:T(8,128)S(1)}, u32[]{:S(2)}, u32[]{:S(2)}) collective-permute-start(f32[8,256]{1,0:T(8,128)S(1)} %concatenate.3), channel_id=1, source_target_pairs={{0,16},{16,0},{32,48},{48,32},{64,80},{80,64},{96,112},{112,96},{1... | collective-permute-start | bytes 24584 | tf_op jit(solution)/shard_map/ppermute | solution.py:235
  5.3 11.8 %collective-permute-start.1 = (f32[8,256]{1,0:T(8,128)S(1)}, f32[8,256]{1,0:T(8,128)S(1)}, u32[]{:S(2)}, u32[]{:S(2)}) collective-permute-start(f32[8,256]{1,0:T(8,128)S(1)} %concatenate.3), channel_id=1, source_target_pairs={{0,32},{16,48},{32,0},{48,16},{64,96},{80,112},{96,64},{112,80},{1... | collective-permute-start | bytes 24584 | tf_op jit(solution)/shard_map/ppermute | solution.py:235
  10.4 6.7 %collective-permute-start.2 = (f32[8,256]{1,0:T(8,128)S(1)}, f32[8,256]{1,0:T(8,128)S(1)}, u32[]{:S(2)}, u32[]{:S(2)}) collective-permute-start(f32[8,256]{1,0:T(8,128)S(1)} %concatenate.3), channel_id=1, source_target_pairs={{0,48},{16,32},{32,16},{48,0},{64,112},{80,96},{96,80},{112,64},{1... | collective-permute-start | bytes 24584 | tf_op jit(solution)/shard_map/ppermute | solution.py:235
  15.9 1.0 %copy-start.2 = (s32[2]{0:T(128)S(1)}, s32[2]{0:T(128)}, u32[]{:S(2)}) copy-start(s32[2]{0:T(128)} %param.13) | copy-start | bytes 28
  16.8 7.2 %copy-start = (f32[3,512]{1,0:T(4,128)S(1)}, f32[3,512]{1,0:T(4,128)}, u32[]{:S(2)}) copy-start(f32[3,512]{1,0:T(4,128)} %uvw_ref.1) | copy-start | bytes 18436
  17.1 4.4 %collective-permute-start.4 = (f32[4,8,256]{2,1,0:T(8,128)S(1)}, f32[4,8,256]{2,1,0:T(8,128)S(1)}, u32[]{:S(2)}, u32[]{:S(2)}) collective-permute-start(f32[4,8,256]{2,1,0:T(8,128)S(1)} %get-tuple-element.17), channel_id=1, source_target_pairs={{0,128},{16,144},{32,160},{48,176},{64,192},{80,208},{96,224},{112... | collective-permute-start | bytes 98312 | tf_op jit(solution)/shard_map/ppermute | solution.py:239
  20.1 4.0 %collective-permute-start.5 = (f32[4,8,256]{2,1,0:T(8,128)S(1)}, f32[4,8,256]{2,1,0:T(8,128)S(1)}, u32[]{:S(2)}, u32[]{:S(2)}) collective-permute-start(f32[4,8,256]{2,1,0:T(8,128)S(1)} %get-tuple-element.17), channel_id=1, source_target_pairs={{0,192},{16,208},{32,224},{48,240},{64,128},{80,144},{96,160},{112... | collective-permute-start | bytes 98312 | tf_op jit(solution)/shard_map/ppermute | solution.py:239
  20.9 3.2 %collective-permute-start.3 = (f32[4,8,256]{2,1,0:T(8,128)S(1)}, f32[4,8,256]{2,1,0:T(8,128)S(1)}, u32[]{:S(2)}, u32[]{:S(2)}) collective-permute-start(f32[4,8,256]{2,1,0:T(8,128)S(1)} %get-tuple-element.17), channel_id=1, source_target_pairs={{0,64},{16,80},{32,96},{48,112},{64,0},{80,16},{96,32},{112,48},{1... | collective-permute-start | bytes 98312 | tf_op jit(solution)/shard_map/ppermute | solution.py:239
  45.0 28.9 %all-to-all-start = ((f32[256,1,256]{2,1,0:T(1,128)}), f32[256,1,256]{2,1,0:T(1,128)S(1)}, u32[]{:S(2)}, u32[]{:S(2)}) async-start(f32[256,1,256]{2,1,0:T(1,128)} %get-tuple-element.5), calls=%async_computation | async-start | bytes 524288 | tf_op jit(solution)/shard_map/all_to_all | solution.py:269
  58.5 15.7 %copy-start.1 = (f32[256]{0:T(256)S(1)}, f32[256]{0:T(256)}, u32[]{:S(2)}) copy-start(f32[256]{0:T(256)} %param.11) | copy-start | bytes 3076

commit v3 on v2

--- a/solution.py
+++ b/solution.py
@@ -11,7 +11,7 @@
 NB = 32
 GROUP = 8
 CHUNK = 512
-ROWS = 64
+ROWS = 256
 SIN_COEF = tuple(
     k * (1.0 - 2.0e-6) for k in (3.14158202, -5.16714276, 2.54189867, -0.55463514)
 )
@@ -25,8 +25,16 @@
     return hi, mid, low
 
 
+def weave(*parts):
+    parts = list(parts)
+    while parts:
+        for part in list(parts):
+            if next(part, parts) is parts:
+                parts.remove(part)
+
+
 def kernel(
-    ib_ref, jb_ref, dest_ref, ratio_ref, uvw_ref, d_ref, ref_ref, res_ref, sent_ref, lhs_ref, acc_ref, *rest
+    ib_ref, jb_ref, ratio_ref, uvw_ref, d_ref, ref_ref, res_ref, sent_ref, lhs_ref, acc_ref, *rest
 ):
     chans, slots, two, side = ref_ref.shape
     blocks, _, width = d_ref.shape
@@ -84,6 +92,7 @@
             b = r // side
             q_ref[b : b + ROWS // side, 0:side] = re
             q_ref[b : b + ROWS // side, side:two] = im
+            yield
 
     def model(ch, step):
         q_ref = q_refs[ch * steps + step]
@@ -100,6 +109,7 @@
                 p_ref[0:size, 0:size] = part
             else:
                 p_ref[0:size, 0:size] += part
+            yield
 
     def residuals(ch):
         lane = lax.broadcasted_iota(jnp.int32, (two, 128), 1)
@@ -144,6 +154,7 @@
             )
             m = stack(q_ref, ib_ref, first, count).astype(jnp.float32) * m
             acc = acc + jnp.sum(m.reshape(size // 8, 8, CHUNK), axis=0)
+            yield
         if ch > 0:
             acc = acc + acc_ref[step]
         if ch < chans - 1:
@@ -152,32 +163,34 @@
         total = jnp.sum(acc, axis=0, keepdims=True)
         for k in range(per):
             line = total[:, k * width : (k + 1) * width]
-            sent_ref[pl.ds(dest_ref[step * per + k] * copies, copies)] = jnp.broadcast_to(
-                line[None], (copies, 1, width)
-            )
+            first = (step * per + k) * copies
+            sent_ref[first : first + copies] = jnp.broadcast_to(line[None], (copies, 1, width))
 
     for ch in range(chans):
         stations_of(ch)
     for ch in range(chans):
         for step in range(steps):
-            phasors(ch, step)
             if step > 0:
-                model(ch, step - 1)
+                beside = [model(ch, step - 1)]
                 if ch > 0:
-                    gradient(ch - 1, step - 1)
+                    beside.append(gradient(ch - 1, step - 1))
+                weave(phasors(ch, step), *beside)
             elif ch > 0:
-                model(ch - 1, steps - 1)
+                weave(phasors(ch, step), model(ch - 1, steps - 1))
                 residuals(ch - 1)
+            else:
+                weave(phasors(ch, step))
     last = chans - 1
-    model(last, steps - 1)
     if last > 0:
-        gradient(last - 1, steps - 1)
+        weave(model(last, steps - 1), gradient(last - 1, steps - 1))
+    else:
+        weave(model(last, steps - 1))
     residuals(last)
     for step in range(steps):
-        gradient(last, step)
-
-
-def device_kernel(ib, jb, dest, ratio, uvw, d, ref, copies):
+        weave(gradient(last, step))
+
+
+def device_kernel(ib, jb, ratio, uvw, d, ref, copies):
     chans, slots, two, _ = ref.shape
     blocks, _, width = d.shape
     stations = uvw.shape[1]
@@ -192,7 +205,7 @@
             jax.ShapeDtypeStruct(ref.shape, jnp.float32),
             jax.ShapeDtypeStruct((blocks * copies, 1, width), jnp.float32),
         ),
-        in_specs=[sm, sm, sm, sm, vm, vm, vm],
+        in_specs=[sm, sm, sm, vm, vm, vm],
         out_specs=(vm, vm),
         scratch_shapes=[
             pltpu.VMEM((chans, stations, 48), jnp.bfloat16),
@@ -203,7 +216,7 @@
         + [pltpu.VMEM((NB, two, CHUNK), jnp.bfloat16)] * (chans * steps),
         compiler_params=pltpu.CompilerParams(vmem_limit_bytes=48 * 2**20),
         name="visibility",
-    )(ib, jb, dest, ratio, uvw, d, ref)
+    )(ib, jb, ratio, uvw, d, ref)
 
 
 def slot_tables(own_pairs):
@@ -222,22 +235,6 @@
     herm = jnp.stack([part[:, :, 0] + turned[:, :, 0], part[:, :, 1] - turned[:, :, 1]], axis=2)
     out = jnp.where(on_diag[None, :, None, None, None], herm, shaped)
     return out.reshape(chans, slots, 2 * side, side)
-
-
-def swap_perm(count, k):
-    return [(i, i ^ k) for i in range(count)]
-
-
-def gather_components(own, count):
-    me = lax.axis_index("comp")
-    parts = {0: own}
-    for k in (1, 2, 3):
-        parts[k] = lax.ppermute(own, "comp", swap_perm(count, k))
-    low = jnp.stack([parts[k] for k in range(4)], axis=0)
-    rounds = {0: low}
-    for k in (4, 8, 12):
-        rounds[k] = lax.ppermute(low, "comp", swap_perm(count, k))
-    return jnp.stack([rounds[k] for k in (0, 4, 8, 12)], axis=0)
 
 
 def body(station_uvw, directions, flux_ref, spectral_index, channel_index, slot_pair, observed):
@@ -253,18 +250,18 @@
     me = lax.axis_index("comp")
     ratios = 1.0 + channel_index.astype(jnp.float32) / 4096.0
 
-    blank = jnp.zeros((3, per_block), jnp.float32)
+    rows = [directions, jnp.zeros((1, per_block), jnp.float32), flux_ref[None], spectral_index[None]]
+    rows.append(jnp.zeros((8 - 5, per_block), jnp.float32))
     own = jnp.concatenate(
-        [directions, blank[:1], flux_ref[None], spectral_index[None], blank], axis=0
+        [jnp.broadcast_to(row[None], (comp_count,) + row.shape) for row in rows], axis=1
     )
-    d = gather_components(own, comp_count).reshape(comp_count, 8, per_block)
-    dest = me ^ jnp.arange(comp_count, dtype=jnp.int32)
+    d = lax.all_to_all(own, "comp", 0, 0, tiled=True)
     ratio = jnp.stack([ratios, jnp.log2(ratios)], axis=0)
 
     own_pairs = lax.dynamic_slice_in_dim(slot_pair, me * own_slots, own_slots)
     ib, jb = slot_tables(own_pairs)
     ref = reference_blocks(observed, ib == jb, side)
-    res, sent = device_kernel(ib, jb, dest, ratio, station_uvw, d, ref, group_count)
+    res, sent = device_kernel(ib, jb, ratio, station_uvw, d, ref, group_count)
     residual = res.reshape(chans, own_slots, 2 * side * side)
     got = lax.all_to_all(sent, ("comp", "freq"), 0, 0, tiled=True)
     flux_grad = jnp.sum(got, axis=(0, 1)) / (flux_ref * (scale * stations * chans * group_count))

time: 75.1 us -> 71.3 us (0.949)
  starting transfers between devices: 26.3 us -> 22.3 us
  local copies, waits for them, and re-layouts: 6.29 us -> 8.54 us
  Pallas kernels: 20.9 us -> 19.1 us
    ppermute x6 -> x0, starting transfers between devices: 12.8 us -> none  [the longest x3 9.02 us: gather_components(): parts[k] = lax.ppermute(own, 'comp', swap_perm(count, k))]
    all_to_all x0 -> x1, starting transfers between devices: none -> 11.7 us  [body(): d = lax.all_to_all(own, 'comp', 0, 0, tiled=True)]
    all_to_all x0 -> x1, waiting for transfers between devices: none -> 3.43 us  [body(): d = lax.all_to_all(own, 'comp', 0, 0, tiled=True)]
    ppermute x6 -> x0, waiting for transfers between devices: 3.2 us -> none  [the longest x3 3.2 us: gather_components(): rounds[k] = lax.ppermute(low, 'comp', swap_perm(count, k))]
    all_to_all x1, starting transfers between devices: 13.5 us -> 10.6 us  [body(): got = lax.all_to_all(sent, ('comp', 'freq'), 0, 0, tiled=True)]
    broadcast_in_dim x1 -> x3, local copies, waits for them, and re-layouts: 0.01 us -> 2.08 us  [body(): jnp.broadcast_to(row[None], (comp_count,) + row.shape)]
    pallas_call x1, Pallas kernels: 20.9 us -> 19.1 us  [device_kernel(): pl.pallas_call(kernel, out_shape=(jax.ShapeDtypeStruct(ref.shape, jnp.flo...]
    unnamed x8 -> x10, local copies, waits for them, and re-layouts: 1.99 us -> 2 us
  transfers between devices with their start and end apart: 7 -> 2, of which waited for: 3 -> 2; matrix products, arithmetic and copies ran while one was open for 11% -> 11% of each run, Pallas kernels for 0% -> 0%
where the time goes in v3:
time: 71.3 us; the launch traced here: 70.8 us
  starting transfers between devices  22.3 us (31%)
  Pallas kernels  19.1 us (27%)
  waiting for transfers between devices  17.3 us (24%)
  local copies, waits for them, and re-layouts  8.54 us (12%)
  other arithmetic  2.78 us (4%)
  between operations  0.79 us (1%)
    pallas_call x1, Pallas kernels, device_kernel(): pl.pallas_call(kernel, out_shape=(jax.ShapeDtypeStruct(ref.shape, jnp.flo...  19.1 us
    all_to_all x1, waiting for transfers between devices, body(): got = lax.all_to_all(sent, ('comp', 'freq'), 0, 0, tiled=True)  13.9 us
    all_to_all x1, starting transfers between devices, body(): d = lax.all_to_all(own, 'comp', 0, 0, tiled=True)  11.7 us
    all_to_all x1, starting transfers between devices, body(): got = lax.all_to_all(sent, ('comp', 'freq'), 0, 0, tiled=True)  10.6 us
    all_to_all x1, waiting for transfers between devices, body(): d = lax.all_to_all(own, 'comp', 0, 0, tiled=True)  3.43 us
    broadcast_in_dim x3, local copies, waits for them, and re-layouts, body(): jnp.broadcast_to(row[None], (comp_count,) + row.shape)  2.08 us
    unnamed x10, local copies, waits for them, and re-layouts  2 us
  transfers between devices with their start and end apart: 2, of which 2 were waited for; matrix products, arithmetic and copies ran while one was open for 11% of the time, Pallas kernels for 0%

profile of v3, /device:TPU:1, one launch (start us, length us, event | category | flops | bytes accessed | tf_op | source)
XLA Modules:
  0.0 70.8 jit_solution(11443472180242070242)
XLA Ops:
  0.6 0.0 copy-start.2
  0.6 0.7 broadcast_in_dim.19
  1.3 0.7 broadcast_in_dim.36
  2.0 0.7 broadcast_in_dim.37
  2.8 0.8 %concatenate.3 = f32[16,8,256]{2,1,0:T(8,128)} concatenate(f32[16,2,256]{2,1,0:T(2,128)S(1)} %broadcast_in_dim.19, f32[16,1,256]{2,1,0:T(1,128)S(1)} %broadcast_in_dim_broadcast_in_dim_broadcast_in_dim.6, f32[16,1,256]{2,1,0:T(1,128)S(1)} %broadcast_in_dim.36, f32[16,1,256]{2,1,0:T(1,128)S(1)} %broadcast_in_dim.37, f32[16,3,256]{2,1,0:T(4,128)S(1)} %broadcast_in_dim_broadcast_in_dim_broadcast_in_dim.7), dimensions={1} | concatenate | bytes 262144 | tf_op jit(solution)/shard_map/concatenate | solution.py:255
  3.5 11.7 %all-to-all-start = ((f32[16,8,256]{2,1,0:T(8,128)}), f32[16,8,256]{2,1,0:T(8,128)S(1)}, u32[]{:S(2)}, u32[]{:S(2)}) async-start(f32[16,8,256]{2,1,0:T(8,128)} %concatenate.3), calls=%async_computation | async-start | bytes 262144 | tf_op jit(solution)/shard_map/all_to_all | solution.py:258
  15.3 0.8 %dynamic_slice.3 = s32[33]{0:T(128)S(1)} dynamic-slice(s32[528]{0:T(1024)} %param.14, s32[]{:T(128)S(6)} %select_n.17), dynamic_slice_sizes={33} | dynamic-slice | bytes 268 | tf_op jit(solution)/shard_map/dynamic_slice | solution.py:261
  16.1 0.7 %convert_reduce_fusion = s32[33]{0:T(128)S(1)} fusion(s32[33]{0:T(128)S(1)} %dynamic_slice.3, s32[32]{0:T(128)} %constant.48.clone), kind=kLoop, calls=%fused_computation.6 | loop fusion | flops 3135 | bytes 392 | tf_op jit(solution)/shard_map/reduce_sum | solution.py:224
  16.8 0.8 %fusion.1 = (pred[33]{0:T(512)(128)(4,1)S(1)}, s32[33]{0:T(128)S(1)}) fusion(s32[33]{0:T(128)S(1)} %convert_reduce_fusion, s32[528]{0:T(1024)} %param.14, s32[]{:T(128)S(6)} %select_n.17), kind=kLoop, calls=%fused_computation.18 | loop fusion | flops 759 | bytes 433 | tf_op jit(solution)/shard_map/eq | solution.py:263
  17.6 1.1 %copy.22 = f32[2,33,512]{1,2,0:T(8,128)S(1)} copy(f32[2,33,512]{2,0,1:T(2,128)} %param.15) | data formatting | bytes 270336 | tf_op args[6]
  18.7 0.0 copy-done.2
  18.7 0.1 broadcast_select_fusion
  18.8 0.2 copy.30
  19.0 0.1 slice_add_fusion
  19.1 1.0 %copy.24 = f32[2,33,2,16,16]{4,3,2,1,0:T(8,128)S(1)} copy(f32[2,33,2,16,16]{1,4,3,2,0:T(8,128)S(1)} %pad_maximum_fusion) | data formatting | bytes 270336 | tf_op jit(solution)/shard_map/stack | solution.py:235
  20.1 0.0 copy-start.3
  20.1 1.0 %copy.26 = f32[2,33,32,16]{3,2,1,0:T(8,128)S(1)} copy(f32[2,33,32,16]{1,3,2,0:T(8,128)S(1)} %bitcast.13) | data formatting | bytes 270336 | tf_op jit(solution)/shard_map/reshape | solution.py:231
  21.2 0.0 copy-done.3
  21.2 0.0 copy-start
  21.2 0.2 bitcast_select_fusion.ref_ref
  21.4 3.4 %all-to-all-done.d_ref = f32[16,8,256]{2,1,0:T(8,128)S(1)} async-done(((f32[16,8,256]{2,1,0:T(8,128)}), f32[16,8,256]{2,1,0:T(8,128)S(1)}, u32[]{:S(2)}, u32[]{:S(2)}) %all-to-all-start) | async-done | bytes 131104 | tf_op jit(solution)/shard_map/all_to_all | solution.py:258
  24.8 0.0 copy-done
  24.8 19.1 %visibility.1 = (f32[2,33,32,16]{3,2,1,0:T(8,128)S(1)}, f32[256,1,256]{2,1,0:T(1,128)}) custom-call(s32[33]{0:T(128)S(1)} %broadcast_add_fusion.ib_ref, s32[33]{0:T(128)S(1)} %get-tuple-element.13.jb_ref, f32[2,2]{1,0:T(2,128)S(1)} %pad_maximum_fusion.1.ratio_ref, f32[3,512]{1,0:T(4,128)S(1)} %copy-done, f32[16,8,256]{2,1,0:T(8,128)S(1)} %all-to-all-done.d_ref, ...), custom_call_target="tpu_custom_call" | custom-call | tf_op jit(solution)/shard_map/visibility/pallas_call | solution.py:202
  44.0 10.6 %all-to-all-start.1 = ((f32[256,1,256]{2,1,0:T(1,128)}), f32[256,1,256]{2,1,0:T(1,128)S(1)}, u32[]{:S(2)}, u32[]{:S(2)}) async-start(f32[256,1,256]{2,1,0:T(1,128)} %get-tuple-element.5), calls=%async_computation.1 | async-start | bytes 524288 | tf_op jit(solution)/shard_map/all_to_all | solution.py:266
  54.5 0.0 copy-start.1
  54.5 0.7 %copy.27 = f32[2,33,32,16]{1,3,2,0:T(8,128)S(1)} copy(f32[2,33,32,16]{3,2,1,0:T(8,128)S(1)} %get-tuple-element.4) | data formatting | bytes 270336 | tf_op jit(solution)/shard_map/visibility/pallas_call | solution.py:202
  55.3 0.9 %copy.28 = f32[2,33,512]{2,0,1:T(2,128)} copy(f32[2,33,512]{1,2,0:T(8,128)S(1)} %bitcast.14) | data formatting | bytes 270336
  56.1 13.9 %all-to-all-done.1 = f32[256,1,256]{2,1,0:T(1,128)S(1)} async-done(((f32[256,1,256]{2,1,0:T(1,128)}), f32[256,1,256]{2,1,0:T(1,128)S(1)}, u32[]{:S(2)}, u32[]{:S(2)}) %all-to-all-start.1) | async-done | bytes 262176 | tf_op jit(solution)/shard_map/all_to_all | solution.py:266
  70.0 0.3 reduce_sum.19
  70.3 0.0 copy-done.1
  70.3 0.6 multiply_divide_fusion
  (6 shorter events, 0.1 us)
Async XLA Ops:
  0.6 18.1 %copy-start.2 = (pred[16,16]{1,0:T(8,128)(4,1)S(1)}, pred[16,16]{1,0:T(8,128)(4,1)}, u32[]{:S(2)}) copy-start(pred[16,16]{1,0:T(8,128)(4,1)} %constant.49.clone) | copy-start | bytes 772
  3.5 21.3 %all-to-all-start = ((f32[16,8,256]{2,1,0:T(8,128)}), f32[16,8,256]{2,1,0:T(8,128)S(1)}, u32[]{:S(2)}, u32[]{:S(2)}) async-start(f32[16,8,256]{2,1,0:T(8,128)} %concatenate.3), calls=%async_computation | async-start | bytes 262144 | tf_op jit(solution)/shard_map/all_to_all | solution.py:258
  20.1 1.0 %copy-start.3 = (s32[2]{0:T(128)S(1)}, s32[2]{0:T(128)}, u32[]{:S(2)}) copy-start(s32[2]{0:T(128)} %param.13) | copy-start | bytes 28
  21.2 3.7 %copy-start = (f32[3,512]{1,0:T(4,128)S(1)}, f32[3,512]{1,0:T(4,128)}, u32[]{:S(2)}) copy-start(f32[3,512]{1,0:T(4,128)} %uvw_ref.1) | copy-start | bytes 18436
  44.0 26.0 %all-to-all-start.1 = ((f32[256,1,256]{2,1,0:T(1,128)}), f32[256,1,256]{2,1,0:T(1,128)S(1)}, u32[]{:S(2)}, u32[]{:S(2)}) async-start(f32[256,1,256]{2,1,0:T(1,128)} %get-tuple-element.5), calls=%async_computation.1 | async-start | bytes 524288 | tf_op jit(solution)/shard_map/all_to_all | solution.py:266
  54.5 15.7 %copy-start.1 = (f32[256]{0:T(256)S(1)}, f32[256]{0:T(256)}, u32[]{:S(2)}) copy-start(f32[256]{0:T(256)} %param.11) | copy-start | bytes 3076

commit v4 on v3

--- a/solution.py
+++ b/solution.py
@@ -152,15 +152,18 @@
                 stack(q_ref, jb_ref, first, count),
                 preferred_element_type=jnp.float32,
             )
-            m = stack(q_ref, ib_ref, first, count).astype(jnp.float32) * m
-            acc = acc + jnp.sum(m.reshape(size // 8, 8, CHUNK), axis=0)
+            m = stack(q_ref, ib_ref, first, count) * m.astype(jnp.bfloat16)
+            m = m.reshape(size // 32, 2, 16, CHUNK)
+            m = (m[:, 0] + m[:, 1]).astype(jnp.float32)
+            acc = acc + jnp.sum(m.reshape(size // 16, 8, CHUNK), axis=0)
             yield
         if ch > 0:
             acc = acc + acc_ref[step]
         if ch < chans - 1:
             acc_ref[step] = acc
             return
-        total = jnp.sum(acc, axis=0, keepdims=True)
+        flux = jnp.concatenate([d_ref[step * per + k][3:4] for k in range(per)], axis=1)
+        total = jnp.sum(acc, axis=0, keepdims=True) / (flux * (scale * stations * chans * copies))
         for k in range(per):
             line = total[:, k * width : (k + 1) * width]
             first = (step * per + k) * copies
@@ -245,17 +248,21 @@
     chans = channel_index.shape[0]
     own_slots = observed.shape[1]
     per_block = directions.shape[1]
-    total = per_block * comp_count
-    scale = 1.0 / math.sqrt(total)
     me = lax.axis_index("comp")
     ratios = 1.0 + channel_index.astype(jnp.float32) / 4096.0
 
-    rows = [directions, jnp.zeros((1, per_block), jnp.float32), flux_ref[None], spectral_index[None]]
-    rows.append(jnp.zeros((8 - 5, per_block), jnp.float32))
     own = jnp.concatenate(
-        [jnp.broadcast_to(row[None], (comp_count,) + row.shape) for row in rows], axis=1
+        [
+            directions,
+            jnp.zeros((1, per_block), jnp.float32),
+            flux_ref[None],
+            spectral_index[None],
+            jnp.zeros((3, per_block), jnp.float32),
+        ],
+        axis=0,
     )
-    d = lax.all_to_all(own, "comp", 0, 0, tiled=True)
+    copies = lax.optimization_barrier(jnp.broadcast_to(own[None], (comp_count,) + own.shape))
+    d = lax.all_to_all(copies, "comp", 0, 0, tiled=True)
     ratio = jnp.stack([ratios, jnp.log2(ratios)], axis=0)
 
     own_pairs = lax.dynamic_slice_in_dim(slot_pair, me * own_slots, own_slots)
@@ -264,7 +271,7 @@
     res, sent = device_kernel(ib, jb, ratio, station_uvw, d, ref, group_count)
     residual = res.reshape(chans, own_slots, 2 * side * side)
     got = lax.all_to_all(sent, ("comp", "freq"), 0, 0, tiled=True)
-    flux_grad = jnp.sum(got, axis=(0, 1)) / (flux_ref * (scale * stations * chans * group_count))
+    flux_grad = jnp.sum(got, axis=(0, 1))
     return residual, flux_grad
 
 

time: 71.3 us -> 69.4 us (0.973)
  local copies, waits for them, and re-layouts: 8.54 us -> 7.06 us
    broadcast_in_dim x3, local copies, waits for them, and re-layouts: 2.08 us -> 0.67 us  [the longest x1 0.67 us: body(): jnp.broadcast_to(own[None], (comp_count,) + own.shape)]
    unnamed x10 -> x8, local copies, waits for them, and re-layouts: 2 us -> 1.99 us
where the time goes in v4:
time: 69.4 us; the launch traced here: 69 us
  starting transfers between devices  22.3 us (32%)
  Pallas kernels  18.8 us (27%)
  waiting for transfers between devices  17.3 us (25%)
  local copies, waits for them, and re-layouts  7.06 us (10%)
  other arithmetic  2.77 us (4%)
  between operations  0.78 us (1%)
    pallas_call x1, Pallas kernels, device_kernel(): pl.pallas_call(kernel, out_shape=(jax.ShapeDtypeStruct(ref.shape, jnp.flo...  18.8 us
    all_to_all x1, waiting for transfers between devices, body(): got = lax.all_to_all(sent, ('comp', 'freq'), 0, 0, tiled=True)  13.9 us
    all_to_all x1, starting transfers between devices, body(): d = lax.all_to_all(copies, 'comp', 0, 0, tiled=True)  11.7 us
    all_to_all x1, starting transfers between devices, body(): got = lax.all_to_all(sent, ('comp', 'freq'), 0, 0, tiled=True)  10.6 us
    all_to_all x1, waiting for transfers between devices, body(): d = lax.all_to_all(copies, 'comp', 0, 0, tiled=True)  3.43 us
    unnamed x8, local copies, waits for them, and re-layouts  1.99 us
  transfers between devices with their start and end apart: 2, of which 2 were waited for; matrix products, arithmetic and copies ran while one was open for 11% of the time, Pallas kernels for 0%

profile of v4, /device:TPU:1, one launch (start us, length us, event | category | flops | bytes accessed | tf_op | source)
XLA Modules:
  0.0 69.0 jit_solution(15011250723050892206)
XLA Ops:
  0.6 0.0 copy-start.1
  0.7 0.7 %concatenate.3 = f32[8,256]{1,0:T(8,128)S(1)} concatenate(f32[2,256]{1,0:T(2,128)} %param.10, f32[1,256]{1,0:T(1,128)S(1)} %broadcast_in_dim.37, f32[1,256]{1,0:T(1,128)} %bitcast.18, f32[1,256]{1,0:T(1,128)} %bitcast.19, f32[3,256]{1,0:T(4,128)S(1)} %broadcast_in_dim.40), dimensions={0} | concatenate | bytes 16384 | tf_op jit(solution)/shard_map/concatenate | solution.py:254
  1.4 0.7 broadcast_in_dim.41
  2.1 11.7 %all-to-all-start = ((f32[16,8,256]{2,1,0:T(8,128)}), f32[16,8,256]{2,1,0:T(8,128)S(1)}, u32[]{:S(2)}, u32[]{:S(2)}) async-start(f32[16,8,256]{2,1,0:T(8,128)} %broadcast_in_dim.41), calls=%async_computation | async-start | bytes 262144 | tf_op jit(solution)/shard_map/all_to_all | solution.py:265
  13.8 0.8 %dynamic_slice.3 = s32[33]{0:T(128)S(1)} dynamic-slice(s32[528]{0:T(1024)} %param.14, s32[]{:T(128)S(6)} %select_n.17), dynamic_slice_sizes={33} | dynamic-slice | bytes 268 | tf_op jit(solution)/shard_map/dynamic_slice | solution.py:268
  14.6 0.7 %convert_reduce_fusion = s32[33]{0:T(128)S(1)} fusion(s32[33]{0:T(128)S(1)} %dynamic_slice.3, s32[32]{0:T(128)} %constant.46.clone), kind=kLoop, calls=%fused_computation.6 | loop fusion | flops 3135 | bytes 392 | tf_op jit(solution)/shard_map/reduce_sum | solution.py:227
  15.3 0.8 %fusion.1 = (pred[33]{0:T(512)(128)(4,1)S(1)}, s32[33]{0:T(128)S(1)}) fusion(s32[33]{0:T(128)S(1)} %convert_reduce_fusion, s32[528]{0:T(1024)} %param.14, s32[]{:T(128)S(6)} %select_n.17), kind=kLoop, calls=%fused_computation.17 | loop fusion | flops 759 | bytes 433 | tf_op jit(solution)/shard_map/eq | solution.py:270
  16.1 1.1 %copy.22 = f32[2,33,512]{1,2,0:T(8,128)S(1)} copy(f32[2,33,512]{2,0,1:T(2,128)} %param.15) | data formatting | bytes 270336 | tf_op args[6]
  17.2 0.0 copy-done.1
  17.2 0.1 broadcast_select_fusion
  17.4 0.2 copy.30
  17.5 0.1 slice_add_fusion
  17.7 1.0 %copy.24 = f32[2,33,2,16,16]{4,3,2,1,0:T(8,128)S(1)} copy(f32[2,33,2,16,16]{1,4,3,2,0:T(8,128)S(1)} %pad_maximum_fusion) | data formatting | bytes 270336 | tf_op jit(solution)/shard_map/stack | solution.py:238
  18.7 0.0 copy-start.2
  18.7 1.0 %copy.26 = f32[2,33,32,16]{3,2,1,0:T(8,128)S(1)} copy(f32[2,33,32,16]{1,3,2,0:T(8,128)S(1)} %bitcast.15) | data formatting | bytes 270336 | tf_op jit(solution)/shard_map/reshape | solution.py:234
  19.7 0.0 copy-done.2
  19.7 0.0 copy-start
  19.7 0.2 bitcast_select_fusion.ref_ref
  19.9 3.4 %all-to-all-done.d_ref = f32[16,8,256]{2,1,0:T(8,128)S(1)} async-done(((f32[16,8,256]{2,1,0:T(8,128)}), f32[16,8,256]{2,1,0:T(8,128)S(1)}, u32[]{:S(2)}, u32[]{:S(2)}) %all-to-all-start) | async-done | bytes 131104 | tf_op jit(solution)/shard_map/all_to_all | solution.py:265
  23.4 0.0 copy-done
  23.4 18.8 %visibility.1 = (f32[2,33,32,16]{3,2,1,0:T(8,128)S(1)}, f32[256,1,256]{2,1,0:T(1,128)}) custom-call(s32[33]{0:T(128)S(1)} %broadcast_add_fusion.ib_ref, s32[33]{0:T(128)S(1)} %get-tuple-element.13.jb_ref, f32[2,2]{1,0:T(2,128)S(1)} %pad_maximum_fusion.1.ratio_ref, f32[3,512]{1,0:T(4,128)S(1)} %copy-done, f32[16,8,256]{2,1,0:T(8,128)S(1)} %all-to-all-done.d_ref, ...), custom_call_target="tpu_custom_call" | custom-call | tf_op jit(solution)/shard_map/visibility/pallas_call | solution.py:205
  42.1 10.6 %all-to-all-start.1 = ((f32[256,1,256]{2,1,0:T(1,128)}), f32[256,1,256]{2,1,0:T(1,128)S(1)}, u32[]{:S(2)}, u32[]{:S(2)}) async-start(f32[256,1,256]{2,1,0:T(1,128)} %get-tuple-element.5), calls=%async_computation.1 | async-start | bytes 524288 | tf_op jit(solution)/shard_map/all_to_all | solution.py:273
  52.7 0.7 %copy.27 = f32[2,33,32,16]{1,3,2,0:T(8,128)S(1)} copy(f32[2,33,32,16]{3,2,1,0:T(8,128)S(1)} %get-tuple-element.4) | data formatting | bytes 270336 | tf_op jit(solution)/shard_map/visibility/pallas_call | solution.py:205
  53.4 0.9 %copy.28 = f32[2,33,512]{2,0,1:T(2,128)} copy(f32[2,33,512]{1,2,0:T(8,128)S(1)} %bitcast.16) | data formatting | bytes 270336
  54.3 13.9 %all-to-all-done.1 = f32[256,1,256]{2,1,0:T(1,128)S(1)} async-done(((f32[256,1,256]{2,1,0:T(1,128)}), f32[256,1,256]{2,1,0:T(1,128)S(1)}, u32[]{:S(2)}, u32[]{:S(2)}) %all-to-all-start.1) | async-done | bytes 262176 | tf_op jit(solution)/shard_map/all_to_all | solution.py:273
  68.1 0.8 %reduce_sum.19 = f32[256]{0:T(256)} reduce(f32[256,1,256]{2,1,0:T(1,128)S(1)} %all-to-all-done.1, f32[]{:T(128)} %constant.45.clone.1), dimensions={0,1}, to_apply=%region_1.2 | reduce | flops 65280 | bytes 263172 | tf_op jit(solution)/shard_map/reduce_sum | solution.py:274
  (6 shorter events, 0.1 us)
Async XLA Ops:
  0.6 16.6 %copy-start.1 = (pred[16,16]{1,0:T(8,128)(4,1)S(1)}, pred[16,16]{1,0:T(8,128)(4,1)}, u32[]{:S(2)}) copy-start(pred[16,16]{1,0:T(8,128)(4,1)} %constant.47.clone) | copy-start | bytes 772
  2.1 21.3 %all-to-all-start = ((f32[16,8,256]{2,1,0:T(8,128)}), f32[16,8,256]{2,1,0:T(8,128)S(1)}, u32[]{:S(2)}, u32[]{:S(2)}) async-start(f32[16,8,256]{2,1,0:T(8,128)} %broadcast_in_dim.41), calls=%async_computation | async-start | bytes 262144 | tf_op jit(solution)/shard_map/all_to_all | solution.py:265
  18.7 1.0 %copy-start.2 = (s32[2]{0:T(128)S(1)}, s32[2]{0:T(128)}, u32[]{:S(2)}) copy-start(s32[2]{0:T(128)} %param.13) | copy-start | bytes 28
  19.7 3.7 %copy-start = (f32[3,512]{1,0:T(4,128)S(1)}, f32[3,512]{1,0:T(4,128)}, u32[]{:S(2)}) copy-start(f32[3,512]{1,0:T(4,128)} %uvw_ref.1) | copy-start | bytes 18436
  42.1 26.0 %all-to-all-start.1 = ((f32[256,1,256]{2,1,0:T(1,128)}), f32[256,1,256]{2,1,0:T(1,128)S(1)}, u32[]{:S(2)}, u32[]{:S(2)}) async-start(f32[256,1,256]{2,1,0:T(1,128)} %get-tuple-element.5), calls=%async_computation.1 | async-start | bytes 524288 | tf_op jit(solution)/shard_map/all_to_all | solution.py:273

commit v5 on v4

--- a/solution.py
+++ b/solution.py
@@ -66,10 +66,10 @@
         d = jnp.concatenate([d_ref[step * per + k] for k in range(per)], axis=1)
         l_part, m_part = d[0:1], d[1:2]
         w_term = jnp.sqrt(1.0 - l_part * l_part - m_part * m_part) - 1.0
-        row = lax.broadcasted_iota(jnp.int32, d.shape, 0)
-        hi, mid, low = pieces(jnp.where(row == 2, w_term, d))
+        blank = jnp.zeros((5, CHUNK), jnp.float32)
+        hi, mid, low = pieces(jnp.concatenate([l_part, m_part, w_term, blank], axis=0))
         rhs = jnp.concatenate([hi, mid, low, hi, mid, hi], axis=0).astype(jnp.bfloat16)
-        gain = jnp.sqrt(d[3:4] * jnp.exp2(d[4:5] * ratio_ref[1, ch]) * scale)
+        gain = jnp.sqrt(d[2:3] * jnp.exp2(d[3:4] * ratio_ref[1, ch]) * scale)
         root = jnp.sqrt(2.0 * gain)
         coef = [jnp.broadcast_to(-k * root, (8, CHUNK))[None] for k in SIN_COEF]
         gain1 = jnp.broadcast_to(gain, (8, CHUNK))[None]
@@ -162,7 +162,7 @@
         if ch < chans - 1:
             acc_ref[step] = acc
             return
-        flux = jnp.concatenate([d_ref[step * per + k][3:4] for k in range(per)], axis=1)
+        flux = jnp.concatenate([d_ref[step * per + k][2:3] for k in range(per)], axis=1)
         total = jnp.sum(acc, axis=0, keepdims=True) / (flux * (scale * stations * chans * copies))
         for k in range(per):
             line = total[:, k * width : (k + 1) * width]
@@ -171,7 +171,6 @@
 
     for ch in range(chans):
         stations_of(ch)
-    for ch in range(chans):
         for step in range(steps):
             if step > 0:
                 beside = [model(ch, step - 1)]
@@ -254,10 +253,8 @@
     own = jnp.concatenate(
         [
             directions,
-            jnp.zeros((1, per_block), jnp.float32),
             flux_ref[None],
             spectral_index[None],
-            jnp.zeros((3, per_block), jnp.float32),
         ],
         axis=0,
     )

time: 69.4 us -> 70 us (level)
  other arithmetic: 2.77 us -> 4.18 us
  starting transfers between devices: 22.3 us -> 23.5 us
  waiting for transfers between devices: 17.3 us -> 16.1 us
  local copies, waits for them, and re-layouts: 7.06 us -> 6.29 us
    all_to_all x1, waiting for transfers between devices: 3.43 us -> 2.25 us  [body(): d = lax.all_to_all(copies, 'comp', 0, 0, tiled=True)]
    all_to_all x1, starting transfers between devices: 10.6 us -> 11.7 us  [body(): got = lax.all_to_all(sent, ('comp', 'freq'), 0, 0, tiled=True)]
    concatenate x1 -> x0, local copies, waits for them, and re-layouts: 0.73 us -> none  [body(): jnp.concatenate([directions, jnp.zeros((1, per_block), jnp.float32), flux...]
    concatenate x0 -> x1, other arithmetic: none -> 0.72 us  [body(): jnp.concatenate([directions, flux_ref[None], spectral_index[None]], axis=0)]
    unnamed x8 -> x6, local copies, waits for them, and re-layouts: 1.99 us -> 1.99 us
  transfers between devices with their start and end apart: 2 -> 2, of which waited for: 2 -> 2; matrix products, arithmetic and copies ran while one was open for 11% -> 12% of each run, Pallas kernels for 0% -> 0%
where the time goes in v5:
time: 70 us; the launch traced here: 69.6 us
  starting transfers between devices  23.5 us (34%)
  Pallas kernels  18.8 us (27%)
  waiting for transfers between devices  16.1 us (23%)
  local copies, waits for them, and re-layouts  6.29 us (9%)
  other arithmetic  4.18 us (6%)
  between operations  0.75 us (1%)
    pallas_call x1, Pallas kernels, device_kernel(): pl.pallas_call(kernel, out_shape=(jax.ShapeDtypeStruct(ref.shape, jnp.flo...  18.8 us
    all_to_all x1, waiting for transfers between devices, body(): got = lax.all_to_all(sent, ('comp', 'freq'), 0, 0, tiled=True)  13.9 us
    all_to_all x1, starting transfers between devices, body(): d = lax.all_to_all(copies, 'comp', 0, 0, tiled=True)  11.7 us
    all_to_all x1, starting transfers between devices, body(): got = lax.all_to_all(sent, ('comp', 'freq'), 0, 0, tiled=True)  11.7 us
    all_to_all x1, waiting for transfers between devices, body(): d = lax.all_to_all(copies, 'comp', 0, 0, tiled=True)  2.25 us
    unnamed x6, local copies, waits for them, and re-layouts  1.99 us
  transfers between devices with their start and end apart: 2, of which 2 were waited for; matrix products, arithmetic and copies ran while one was open for 12% of the time, Pallas kernels for 0%

profile of v5, /device:TPU:1, one launch (start us, length us, event | category | flops | bytes accessed | tf_op | source)
XLA Modules:
  0.0 69.6 jit_solution(16510892214742407134)
XLA Ops:
  0.6 0.7 %pad_maximum_fusion.1 = f32[4,256]{1,0:T(4,128)S(1)} fusion(f32[1,256]{1,0:T(1,128)} %bitcast.18, f32[1,256]{1,0:T(1,128)} %bitcast.19, f32[2,256]{1,0:T(2,128)} %param.10), kind=kLoop, calls=%fused_computation.7 | loop fusion | flops 2048 | bytes 8192 | tf_op jit(solution)/shard_map/concatenate | solution.py:253
  1.4 0.6 broadcast_in_dim.33
  2.0 11.7 %all-to-all-start = ((f32[16,4,256]{2,1,0:T(4,128)}), f32[16,4,256]{2,1,0:T(4,128)S(1)}, u32[]{:S(2)}, u32[]{:S(2)}) async-start(f32[16,4,256]{2,1,0:T(4,128)} %broadcast_in_dim.33), calls=%async_computation | async-start | bytes 131072 | tf_op jit(solution)/shard_map/all_to_all | solution.py:262
  13.8 0.8 %dynamic_slice.3 = s32[33]{0:T(128)S(1)} dynamic-slice(s32[528]{0:T(1024)} %param.14, s32[]{:T(128)S(6)} %select_n.17), dynamic_slice_sizes={33} | dynamic-slice | bytes 268 | tf_op jit(solution)/shard_map/dynamic_slice | solution.py:265
  14.5 0.7 %convert_reduce_fusion = s32[33]{0:T(128)S(1)} fusion(s32[33]{0:T(128)S(1)} %dynamic_slice.3, s32[32]{0:T(128)} %constant.44.clone), kind=kLoop, calls=%fused_computation.6 | loop fusion | flops 3135 | bytes 392 | tf_op jit(solution)/shard_map/reduce_sum | solution.py:226
  15.3 0.8 %fusion.1 = (pred[33]{0:T(512)(128)(4,1)S(1)}, s32[33]{0:T(128)S(1)}) fusion(s32[33]{0:T(128)S(1)} %convert_reduce_fusion, s32[528]{0:T(1024)} %param.14, s32[]{:T(128)S(6)} %select_n.17), kind=kLoop, calls=%fused_computation.18 | loop fusion | flops 759 | bytes 433 | tf_op jit(solution)/shard_map/eq | solution.py:267
  16.0 1.1 %copy.22 = f32[2,33,512]{1,2,0:T(8,128)S(1)} copy(f32[2,33,512]{2,0,1:T(2,128)} %param.15) | data formatting | bytes 270336 | tf_op args[6]
  17.2 0.8 %broadcast_select_fusion = f32[2,33,2,16,16]{1,4,3,2,0:T(8,128)S(1)} fusion(f32[2,33,2,16,16]{1,4,3,2,0:T(8,128)S(1)} %bitcast.14, pred[16,16]{1,0:T(8,128)(4,1)} %constant.45.clone), kind=kLoop, calls=%fused_computation.5 | loop fusion | flops 33792 | bytes 270592 | tf_op jit(solution)/shard_map/jit(_where)/select_n | solution.py:235
  18.0 0.2 copy.30
  18.1 0.1 slice_add_fusion
  18.3 1.0 %copy.24 = f32[2,33,2,16,16]{4,3,2,1,0:T(8,128)S(1)} copy(f32[2,33,2,16,16]{1,4,3,2,0:T(8,128)S(1)} %pad_maximum_fusion) | data formatting | bytes 270336 | tf_op jit(solution)/shard_map/stack | solution.py:237
  19.3 0.0 copy-start.1
  19.3 1.0 %copy.26 = f32[2,33,32,16]{3,2,1,0:T(8,128)S(1)} copy(f32[2,33,32,16]{1,3,2,0:T(8,128)S(1)} %bitcast.15) | data formatting | bytes 270336 | tf_op jit(solution)/shard_map/reshape | solution.py:233
  20.3 0.0 copy-done.1
  20.3 0.0 copy-start
  20.3 0.2 bitcast_select_fusion.ref_ref
  20.5 2.3 %all-to-all-done.d_ref = f32[16,4,256]{2,1,0:T(4,128)S(1)} async-done(((f32[16,4,256]{2,1,0:T(4,128)}), f32[16,4,256]{2,1,0:T(4,128)S(1)}, u32[]{:S(2)}, u32[]{:S(2)}) %all-to-all-start) | async-done | bytes 65568 | tf_op jit(solution)/shard_map/all_to_all | solution.py:262
  22.8 0.0 copy-done
  22.8 18.8 %visibility.1 = (f32[2,33,32,16]{3,2,1,0:T(8,128)S(1)}, f32[256,1,256]{2,1,0:T(1,128)}) custom-call(s32[33]{0:T(128)S(1)} %broadcast_add_fusion.ib_ref, s32[33]{0:T(128)S(1)} %get-tuple-element.13.jb_ref, f32[2,2]{1,0:T(2,128)S(1)} %pad_maximum_fusion.2.ratio_ref, f32[3,512]{1,0:T(4,128)S(1)} %copy-done, f32[16,4,256]{2,1,0:T(4,128)S(1)} %all-to-all-done.d_ref, ...), custom_call_target="tpu_custom_call" | custom-call | tf_op jit(solution)/shard_map/visibility/pallas_call | solution.py:204
  41.6 11.7 %all-to-all-start.1 = ((f32[256,1,256]{2,1,0:T(1,128)}), f32[256,1,256]{2,1,0:T(1,128)S(1)}, u32[]{:S(2)}, u32[]{:S(2)}) async-start(f32[256,1,256]{2,1,0:T(1,128)} %get-tuple-element.5), calls=%async_computation.1 | async-start | bytes 524288 | tf_op jit(solution)/shard_map/all_to_all | solution.py:270
  53.3 0.7 %copy.27 = f32[2,33,32,16]{1,3,2,0:T(8,128)S(1)} copy(f32[2,33,32,16]{3,2,1,0:T(8,128)S(1)} %get-tuple-element.4) | data formatting | bytes 270336 | tf_op jit(solution)/shard_map/visibility/pallas_call | solution.py:204
  54.0 0.9 %copy.28 = f32[2,33,512]{2,0,1:T(2,128)} copy(f32[2,33,512]{1,2,0:T(8,128)S(1)} %bitcast.16) | data formatting | bytes 270336
  54.9 13.9 %all-to-all-done.1 = f32[256,1,256]{2,1,0:T(1,128)S(1)} async-done(((f32[256,1,256]{2,1,0:T(1,128)}), f32[256,1,256]{2,1,0:T(1,128)S(1)}, u32[]{:S(2)}, u32[]{:S(2)}) %all-to-all-start.1) | async-done | bytes 262176 | tf_op jit(solution)/shard_map/all_to_all | solution.py:270
  68.8 0.8 %reduce_sum.19 = f32[256]{0:T(256)} reduce(f32[256,1,256]{2,1,0:T(1,128)S(1)} %all-to-all-done.1, f32[]{:T(128)} %constant.43.clone.1), dimensions={0,1}, to_apply=%region_1.2 | reduce | flops 65280 | bytes 263172 | tf_op jit(solution)/shard_map/reduce_sum | solution.py:271
  (4 shorter events, 0.1 us)
Async XLA Ops:
  2.0 20.8 %all-to-all-start = ((f32[16,4,256]{2,1,0:T(4,128)}), f32[16,4,256]{2,1,0:T(4,128)S(1)}, u32[]{:S(2)}, u32[]{:S(2)}) async-start(f32[16,4,256]{2,1,0:T(4,128)} %broadcast_in_dim.33), calls=%async_computation | async-start | bytes 131072 | tf_op jit(solution)/shard_map/all_to_all | solution.py:262
  19.3 1.0 %copy-start.1 = (s32[2]{0:T(128)S(1)}, s32[2]{0:T(128)}, u32[]{:S(2)}) copy-start(s32[2]{0:T(128)} %param.13) | copy-start | bytes 28
  20.3 2.5 %copy-start = (f32[3,512]{1,0:T(4,128)S(1)}, f32[3,512]{1,0:T(4,128)}, u32[]{:S(2)}) copy-start(f32[3,512]{1,0:T(4,128)} %uvw_ref.1) | copy-start | bytes 18436
  41.6 27.2 %all-to-all-start.1 = ((f32[256,1,256]{2,1,0:T(1,128)}), f32[256,1,256]{2,1,0:T(1,128)S(1)}, u32[]{:S(2)}, u32[]{:S(2)}) async-start(f32[256,1,256]{2,1,0:T(1,128)} %get-tuple-element.5), calls=%async_computation.1 | async-start | bytes 524288 | tf_op jit(solution)/shard_map/all_to_all | solution.py:270
